TPU v7x, 256 devices: a whole 4x4x8 slice. The times are simulated.
256 devices in a mesh: rows: 16 (over x, z_hi), cols: 16 (over y, z_lo, core).
Axes of the slice: x: 4, y: 4, z: 8 (z_hi: 4, z_lo: 2; z = z_hi * 2 + z_lo), core: 2. Of those that a mesh axis runs over, the one named last changes fastest.
Arguments:
- features: bfloat16 [512, 512, 128], P('rows', 'cols'), may hold values from -6 to 6
- cotangent: bfloat16 [512, 512, 128], P('rows', 'cols'), may hold values from -6 to 6
- weight: bfloat16 [512, 512], replicated, may hold values from -0.25 to 0.25
- degree: int32 [512, 128], P('rows'), may hold values from 16 to 128
- tile_row: int32 [4096], P('rows'), may hold values from 0 to 31
- tile_col: int32 [4096], P('rows'), may hold values from 0 to 511, as said below
- tile_count: int32 [16], P('rows'), may hold values from 64 to 256, as said below
- tile_weights: bfloat16 [4096, 128, 128], P('rows'), may hold values from 0 to 3
Outputs:
- activated: bfloat16 [512, 512, 128], P('rows', 'cols')
- input_grad: bfloat16 [512, 512, 128], P('rows', 'cols')
- weight_grad: float32 [512, 512], P('cols')
Inputs may be any that keep to these rules, and one draw needn't show every extreme that they name: `tile_col`: within each owner's 256 slots the column blocks never fall. `tile_count`: each owner has 256, 128 or 64 live slots, the first ones of its range; some owner has 256.
All inputs are finite; a program needn't handle non-finite values.
Results may differ from a plain program's by a relative error of at most 0.019.
Values may be sent and summed in bfloat16 or wider, within the bound.
A program may use at most 64 MiB of HBM per device.

v0:
```python
import jax
import jax.numpy as jnp
from jax import lax
from jax.sharding import PartitionSpec as P


def tile_pieces(index, tile_block, first_tile, last_tile, tile_row, tile_col, tile_weights):
    first = index * tile_block
    adjacency = lax.dynamic_slice_in_dim(tile_weights, first, tile_block, 0)
    row_ids = lax.dynamic_slice_in_dim(tile_row, first, tile_block, 0)
    col_ids = lax.dynamic_slice_in_dim(tile_col, first, tile_block, 0)
    place = first + jnp.arange(tile_block, dtype=jnp.int32)
    alive = ((place >= first_tile) & (place < last_tile)).astype(jnp.float32)
    return (adjacency, row_ids, col_ids, alive)


def aggregate(running, source, offset, first_tile, last_tile, tile_row, tile_col, tile_weights):
    tile_block = min(64, tile_col.shape[0])

    def aggregate_advance(index, current):
        adjacency, row_ids, col_ids, alive = tile_pieces(
            index, tile_block, first_tile, last_tile, tile_row, tile_col, tile_weights
        )
        local_ids = jnp.clip(col_ids - offset, 0, source.shape[0] - 1)
        blocks = jnp.take(source, local_ids, axis=0)
        message = jnp.einsum("tfj,tij->tfi", blocks, adjacency, preferred_element_type=jnp.float32)
        return current.at[row_ids].add(message * alive[:, None, None])

    return lax.fori_loop(
        first_tile // tile_block,
        (last_tile + tile_block - 1) // tile_block,
        aggregate_advance,
        running,
    )


def spread_back(
    partial_value, back, offset, first_tile, last_tile, tile_row, tile_col, tile_weights
):
    tile_block = min(64, tile_col.shape[0])

    def spread_advance(index, current):
        adjacency, row_ids, col_ids, alive = tile_pieces(
            index, tile_block, first_tile, last_tile, tile_row, tile_col, tile_weights
        )
        blocks = jnp.take(back, row_ids, axis=0)
        contrib = (
            jnp.einsum("tfi,tij->tfj", blocks, adjacency, preferred_element_type=jnp.float32)
            * alive[:, None, None]
        )
        local_ids = jnp.clip(col_ids - offset, 0, current.shape[0] - 1)
        return current.at[local_ids].add(contrib)

    return lax.fori_loop(
        first_tile // tile_block,
        (last_tile + tile_block - 1) // tile_block,
        spread_advance,
        partial_value,
    )


def body(features, cotangent, weight, degree, tile_row, tile_col, tile_count, tile_weights):
    amount = tile_count[0]
    height, narrow, width = features.shape
    column = lax.axis_index("cols")
    scale = lax.rsqrt(degree.astype(jnp.float32))
    scaled = (features.astype(jnp.float32) * scale[:, None, :]).astype(jnp.bfloat16)
    empty = jnp.zeros((height, narrow, width), jnp.float32)
    gathered = lax.all_gather(scaled, "rows", axis=0, tiled=True)
    aggregated = aggregate(
        empty, gathered, 0, jnp.int32(0), amount, tile_row, tile_col, tile_weights
    )
    hidden = (aggregated * scale[:, None, :]).astype(jnp.bfloat16)
    w_cols = lax.dynamic_slice_in_dim(weight, column * narrow, narrow, 1)
    w_rows = lax.dynamic_slice_in_dim(weight, column * narrow, narrow, 0)
    part_weight = w_cols
    pre = jnp.einsum(
        "bfn,fo->bon",
        lax.all_gather(hidden, "cols", axis=1, tiled=True),
        part_weight,
        preferred_element_type=jnp.float32,
    )
    activated = jax.nn.silu(pre).astype(jnp.bfloat16)
    sigmoid_pre = jax.nn.sigmoid(pre)
    slope = (
        cotangent.astype(jnp.float32) * sigmoid_pre * (1.0 + pre * (1.0 - sigmoid_pre))
    ).astype(jnp.bfloat16)
    portion = lax.all_gather(slope, "cols", axis=1, tiled=True)
    part_weight = w_rows
    back_sum = jnp.einsum("fo,bon->bfn", part_weight, portion, preferred_element_type=jnp.float32)
    grad_part = jnp.einsum("bfn,bon->fo", hidden, portion, preferred_element_type=jnp.float32)
    grad_rows = grad_part
    back_sum, grad_rows = (back_sum, grad_rows)
    weight_grad = lax.psum(grad_rows.astype(jnp.bfloat16), "rows").astype(jnp.float32)
    back = (back_sum * scale[:, None, :]).astype(jnp.bfloat16)
    owners = lax.axis_size("rows")
    blank = jnp.zeros((height * owners, narrow, width), jnp.float32)
    partial_value = spread_back(
        blank, back, 0, jnp.int32(0), amount, tile_row, tile_col, tile_weights
    )
    summed = lax.psum_scatter(
        partial_value.astype(jnp.bfloat16), "rows", scatter_dimension=0, tiled=True
    ).astype(jnp.float32)
    input_grad = (summed * scale[:, None, :]).astype(jnp.bfloat16)
    return (activated, input_grad, weight_grad)


def solution(mesh):
    in_specs = (
        P("rows", "cols", None),
        P("rows", "cols", None),
        P(),
        P("rows", None),
        P("rows"),
        P("rows"),
        P("rows"),
        P("rows", None, None),
    )
    out_specs = (P("rows", "cols", None), P("rows", "cols", None), P("cols", None))
    return jax.shard_map(body, mesh=mesh, in_specs=in_specs, out_specs=out_specs, check_vma=False)
```

profile of v0, /device:TPU:33, one launch (start us, length us, event | category | flops | bytes accessed | tf_op | source)
XLA Modules:
  0.0 384.7 jit_solution(7960542579718967295)
XLA Ops:
  7.2 0.8 convert_rsqrt_fusion
  8.0 1.7 multiply_convert_fusion.4
  10.4 80.3 %all-gather.4.cloned.1.call-done = bf16[512,32,128]{2,1,0:T(8,128)(2,1)} async-done(((bf16[32,32,128]{2,1,0:T(8,128)(2,1)}), bf16[512,32,128]{2,1,0:T(8,128)(2,1)}) %all-gather.4.cloned.1.call-update) | async-done | bytes 4194320 | tf_op jit(solution)/shard_map/all_gather | solution.py:69
  90.8 44.2 %while.20 = (s32[]{:T(128)}, f32[32,32,128]{2,1,0:T(8,128)S(1)}, s32[]{:T(128)}, s32[256]{0:T(256)}, s32[256]{0:T(256)}, /*index=5*/bf16[512,32,128]{2,1,0:T(8,1...) while((s32[]{:T(128)}, f32[32,32,128]{2,1,0:T(8,128)S(1)}, ...), condition=%wide.region_2.3_spmd, body=%wide.region_0.2_spmd.sunk | while | flops 67897288 | bytes 7871031 | solution.py:29
  90.8 0.8 compare_select_fusion.8
  91.6 1.4 compare_and_fusion.4
  93.0 2.8 gather_fusion
  95.9 2.8 fusion.41
  98.7 3.2 scatter_fusion
  101.9 0.8 compare_select_fusion.8
  102.7 1.4 compare_and_fusion.4
  104.1 2.8 gather_fusion
  106.9 2.8 fusion.41
  109.7 3.2 scatter_fusion
  112.9 0.8 compare_select_fusion.8
  113.7 1.4 compare_and_fusion.4
  115.1 2.8 gather_fusion
  118.0 2.8 fusion.41
  120.8 3.2 scatter_fusion
  124.0 0.8 compare_select_fusion.8
  124.7 1.4 compare_and_fusion.4
  126.1 2.8 gather_fusion
  129.0 2.8 fusion.41
  131.8 3.2 scatter_fusion
  135.0 0.8 multiply_convert_fusion.3
  135.8 38.7 %all-gather.6.cloned.1.call-done = bf16[32,512,128]{2,1,0:T(8,128)(2,1)} async-done(((bf16[32,32,128]{2,1,0:T(8,128)(2,1)}), bf16[32,512,128]{2,1,0:T(8,128)(2,1)}) %all-gather.6.cloned.1.call-update) | async-done | bytes 4194320 | tf_op jit(solution)/shard_map/all_gather | solution.py:79
  174.6 4.0 %multiply_convert_fusion.1 = (bf16[32,32,128]{2,1,0:T(8,128)(2,1)}, bf16[32,32,128]{2,1,0:T(8,128)(2,1)}) fusion(bf16[32,32,128]{2,1,0:T(8,128)(2,1)S(1)} %copy-done.2, bf16[32,512,128]{2,1,0:T(8,128)(2,1)} %all-gather.6.cloned.1.call-done, bf16[512,512]{1,0:T(8,128)(2,1)S(1)} %copy-done, s32[]{:T(128)S(6)} %select_n.45), kind=kOutput, calls=%fused_computation.37 | convolution fusion | flops 135790592 | bytes 5111812 | tf_op jit(solution)/shard_map/bfn,fo->bon/dot_general | solution.py:77
  178.6 40.0 %all-gather.8.cloned.1.call-done = bf16[32,512,128]{2,1,0:T(8,128)(2,1)} async-done(((bf16[32,32,128]{2,1,0:T(8,128)(2,1)}), bf16[32,512,128]{2,1,0:T(8,128)(2,1)}) %all-gather.8.cloned.1.call-update) | async-done | bytes 4194320 | tf_op jit(solution)/shard_map/all_gather | solution.py:88
  218.6 3.0 fusion.21
  221.7 4.3 %broadcast_in_dim.43 = f32[512,32,128]{2,1,0:T(8,128)} broadcast(f32[]{:T(128)} %constant.98.clone.1), dimensions={} | broadcast | bytes 8388612 | tf_op jit(solution)/shard_map/broadcast_in_dim | solution.py:97
  226.0 47.4 %while.21 = (s32[]{:T(128)}, f32[512,32,128]{2,1,0:T(8,128)}, s32[]{:T(128)}, s32[256]{0:T(256)S(1)}, s32[256]{0:T(256)S(1)}, /*index=5*/bf16[32,32,128]{2,1,0:T...) while((s32[]{:T(128)}, f32[512,32,128]{2,1,0:T(8,128)}, ...), condition=%wide.region_5.6_spmd, body=%wide.region_3.5_spmd.sunk | while | flops 67897288 | bytes 7871031 | solution.py:54
  226.1 0.7 compare_and_fusion.5
  227.4 2.3 fusion.44
  229.8 8.0 %scatter_fusion.1 = f32[512,32,128]{2,1,0:T(8,128)} fusion(f32[512,32,128]{2,1,0:T(8,128)} %get-tuple-element.292, s32[64]{0:T(128)S(1)} %compare_select_fusion.9, f32[64,32,128]{2,1,0:T(8,128)S(1)} %fusion.44), kind=kCustom, calls=%fused_computation.3.clone.1 | custom fusion | flops 262144 | bytes 3145984 | tf_op jit(solution)/shard_map/while/body/scatter-add | solution.py:52
  237.9 0.7 compare_and_fusion.5
  239.3 2.3 fusion.44
  241.6 8.0 %scatter_fusion.1 = f32[512,32,128]{2,1,0:T(8,128)} fusion(f32[512,32,128]{2,1,0:T(8,128)} %get-tuple-element.292, s32[64]{0:T(128)S(1)} %compare_select_fusion.9, f32[64,32,128]{2,1,0:T(8,128)S(1)} %fusion.44), kind=kCustom, calls=%fused_computation.3.clone.1 | custom fusion | flops 262144 | bytes 3145984 | tf_op jit(solution)/shard_map/while/body/scatter-add | solution.py:52
  249.7 0.7 compare_and_fusion.5
  251.1 2.3 fusion.44
  253.4 8.1 %scatter_fusion.1 = f32[512,32,128]{2,1,0:T(8,128)} fusion(f32[512,32,128]{2,1,0:T(8,128)} %get-tuple-element.292, s32[64]{0:T(128)S(1)} %compare_select_fusion.9, f32[64,32,128]{2,1,0:T(8,128)S(1)} %fusion.44), kind=kCustom, calls=%fused_computation.3.clone.1 | custom fusion | flops 262144 | bytes 3145984 | tf_op jit(solution)/shard_map/while/body/scatter-add | solution.py:52
  262.9 2.3 fusion.44
  265.2 8.1 %scatter_fusion.1 = f32[512,32,128]{2,1,0:T(8,128)} fusion(f32[512,32,128]{2,1,0:T(8,128)} %get-tuple-element.292, s32[64]{0:T(128)S(1)} %compare_select_fusion.9, f32[64,32,128]{2,1,0:T(8,128)S(1)} %fusion.44), kind=kCustom, calls=%fused_computation.3.clone.1 | custom fusion | flops 262144 | bytes 3145984 | tf_op jit(solution)/shard_map/while/body/scatter-add | solution.py:52
  273.3 6.3 %convert_element_type.65 = bf16[512,32,128]{2,1,0:T(8,128)(2,1)} convert(f32[512,32,128]{2,1,0:T(8,128)} %get-tuple-element.90) | non-fusion elementwise | flops 2097152 | bytes 12582912 | tf_op jit(solution)/shard_map/convert_element_type | solution.py:102
  279.7 0.9 copy-done.1
  280.6 3.5 fusion.22
  284.1 66.1 %psum.7 = bf16[32,512]{1,0:T(8,128)(2,1)S(1)} all-reduce(bf16[32,512]{1,0:T(8,128)(2,1)S(1)} %fusion.22), channel_id=1, replica_groups=mesh['rows'=16,'cols'=16] {'rows'}, use_global_device_ids=true, to_apply=%region_7.8 | all-reduce | flops 16384 | bytes 65536 | tf_op jit(solution)/shard_map/psum | solution.py:94
  350.8 25.7 %reduce-scatter.2.cloned.1.call-done = bf16[32,32,128]{2,1,0:T(8,128)(2,1)} async-done(((bf16[512,32,128]{2,1,0:T(8,128)(2,1)}), bf16[32,32,128]{2,1,0:T(8,128)(2,1)}) %reduce-scatter.2.cloned.1.call-update) | async-done | bytes 262160 | tf_op jit(solution)/shard_map/reduce_scatter | solution.py:101
  376.5 1.7 multiply_convert_fusion
  (36 shorter events, 4.6 us)
Async XLA Ops:
  7.2 167.4 %copy-start = (bf16[512,512]{1,0:T(8,128)(2,1)S(1)}, bf16[512,512]{1,0:T(8,128)(2,1)}, u32[]{:S(2)}) copy-start(bf16[512,512]{1,0:T(8,128)(2,1)} %param.14) | copy-start | bytes 1572868
  7.2 83.5 %all-gather.4.cloned.1.call-start = ((), (), s32[]{:S(2)}) async-start(), calls=%async_computation.1 | async-start | bytes 4456448 | tf_op jit(solution)/shard_map/all_gather | solution.py:69
  9.7 164.9 %all-gather.6.cloned.1.call-start = ((), (), s32[]{:S(2)}) async-start(), calls=%async_computation.2 | async-start | bytes 4456448 | tf_op jit(solution)/shard_map/all_gather | solution.py:79
  90.8 83.8 %copy-start.2 = (bf16[32,32,128]{2,1,0:T(8,128)(2,1)S(1)}, bf16[32,32,128]{2,1,0:T(8,128)(2,1)}, u32[]{:S(2)}) copy-start(bf16[32,32,128]{2,1,0:T(8,128)(2,1)} %param.13) | copy-start | bytes 786436
  135.8 82.8 %all-gather.8.cloned.1.call-start = ((), (), s32[]{:S(2)}) async-start(), calls=%async_computation.3 | async-start | bytes 4456448 | tf_op jit(solution)/shard_map/all_gather | solution.py:88
  178.6 197.9 %reduce-scatter.2.cloned.1.call-start = ((), (), s32[]{:S(2)}) async-start(), calls=%async_computation.4 | async-start | bytes 4456448 | tf_op jit(solution)/shard_map/reduce_scatter | solution.py:101
  221.6 4.3 %copy-start.3 = (s32[256]{0:T(256)S(1)}, s32[256]{0:T(256)}, u32[]{:S(2)}) copy-start(s32[256]{0:T(256)} %get-tuple-element.332) | copy-start | bytes 3076
  221.7 4.3 %copy-start.4 = (s32[256]{0:T(256)S(1)}, s32[256]{0:T(256)}, u32[]{:S(2)}) copy-start(s32[256]{0:T(256)} %get-tuple-element.333) | copy-start | bytes 3076
  279.7 0.9 copy-start.1
Sparse Core Ops, SparseCore 0:
  11.0 79.6 all-gather.3
  135.9 38.6 all-gather.5
  178.7 39.8 all-gather.7
  279.8 96.6 reduce-scatter.1
where the time goes:
time: 389 us; the launch traced here: 385 us
  waiting for transfers between devices  185 us (48%)
  other arithmetic  68.7 us (18%)
  blocking collectives  66.1 us (17%)
  matrix products  31 us (8%)
  local copies, waits for them, and re-layouts  19.3 us (5%)
  between operations  14.5 us (4%)
    all_gather x1, waiting for transfers between devices, body(): gathered = lax.all_gather(scaled, 'rows', axis=0, tiled=True)  80.3 us
    psum x1, blocking collectives, body(): lax.psum(grad_rows.astype(jnp.bfloat16), 'rows').astype(jnp.float32)  66.1 us
    all_gather x1, waiting for transfers between devices, body(): portion = lax.all_gather(slope, 'cols', axis=1, tiled=True)  40 us
    all_gather x1, waiting for transfers between devices, body(): lax.all_gather(hidden, 'cols', axis=1, tiled=True)  38.7 us
    scatter-add x4, other arithmetic, spread_advance(): return current.at[local_ids].add(contrib)  32.2 us
    reduce_scatter x1, waiting for transfers between devices, body(): lax.psum_scatter(partial_value.astype(jnp.bfloat16), 'rows', scatter_dime...  25.7 us
    scatter-add x4, other arithmetic, aggregate_advance(): return current.at[row_ids].add(message * alive[:, None, None])  12.6 us
    gather x4, local copies, waits for them, and re-layouts, aggregate_advance(): blocks = jnp.take(source, local_ids, axis=0)  11.4 us
  transfers between devices with their start and end apart: 4, of which 4 were waited for; matrix products, arithmetic and copies ran while one was open for 1% of the time, Pallas kernels for 0%

commit v1 on v0

v1 whole, which is shorter than its diff:
```python
import functools

import jax
import jax.numpy as jnp
from jax import lax
from jax.experimental import pallas as pl
from jax.experimental.pallas import tpu as pltpu
from jax.sharding import PartitionSpec as P

BF = jnp.bfloat16
F32 = jnp.float32
NB = 32
FS = 32
BLK = 128
NX = 4
NZ = 4
NR = NX * NZ
NY = 4
NC = 16
ZFIRST = 24
TB = 16


def rank_along(axis, step):
    r = lax.axis_index("rows")
    x, z = r // NZ, r % NZ
    if axis == "x":
        return ((x + step + NX) % NX) * NZ + z
    return x * NZ + (z + step + NZ) % NZ


def owner_at(first, a, second, b):
    r = lax.axis_index("rows")
    step = {first: a, second: b}
    return ((r // NZ + step["x"] + NX) % NX) * NZ + (r % NZ + step["z"] + NZ) % NZ


class Copies:
    def __init__(self, send, recv):
        self.send, self.recv, self.n, self.started = send, recv, 0, []

    def start(self, src, dst, device):
        k = self.n
        self.n += 1
        c = pltpu.make_async_remote_copy(
            src_ref=src,
            dst_ref=dst,
            send_sem=self.send.at[k],
            recv_sem=self.recv.at[k],
            device_id=device,
            device_id_type=pl.DeviceIdType.MESH,
        )
        c.start()
        self.started.append(c)
        return c

    def finish(self):
        for c in self.started:
            c.wait_send()


def greet(devices):
    barrier = pltpu.get_barrier_semaphore()
    for d in devices:
        pl.semaphore_signal(barrier, inc=1, device_id=d, device_id_type=pl.DeviceIdType.MESH)
    pl.semaphore_wait(barrier, len(devices))


def other_cols():
    c = lax.axis_index("cols")
    return [{"cols": (c + k) % NC} for k in range(1, NC)]


def gather_kernel(feat, deg, cot, w, out, wt, cotx, own, send, recv, lsem):
    me = lax.axis_index("rows")
    c = lax.axis_index("cols")
    peers = [{"rows": rank_along(a, s)} for a in ("x", "z") for s in (1, -1)]
    greet(peers + other_cols())
    copies = Copies(send, recv)

    def scale_block(b, carry):
        s = lax.rsqrt(deg[pl.ds(b, 1), :].astype(F32))
        own[b] = (feat[b].astype(F32) * s).astype(BF)
        return carry

    lax.fori_loop(0, NB, scale_block, 0)
    local = pltpu.make_async_copy(own, out.at[pl.ds(me * NB, NB)], lsem.at[0])
    local.start()

    class Group:
        def __init__(self, first, second, lo, n):
            self.f, self.s, self.lo, self.n = first, second, lo, n

        def blocks(self, a, b, lo, n):
            return pl.ds(owner_at(self.f, a, self.s, b) * NB + self.lo + lo, n)

        def push(self, a, b, lo, n, axis, step):
            ds = self.blocks(a, b, lo, n)
            src = own.at[pl.ds(self.lo + lo, n)] if (a, b) == (0, 0) else out.at[ds]
            return copies.start(src, out.at[ds], {"rows": rank_along(axis, step)})

        def first_start(self):
            self.a_up = self.push(0, 0, 0, self.n, self.f, 1)
            self.a_dn = self.push(0, 0, 0, self.n, self.f, -1)

        def second_start(self, a, lo, n):
            return [a, lo, n, self.push(a, 0, lo, n, self.s, 1), self.push(a, 0, lo, n, self.s, -1)]

        def second_forward(self, item):
            a, lo, n, up, dn = item
            h = n // 2
            up.wait_recv()
            u = self.push(a, -1, lo, h, self.s, 1)
            dn.wait_recv()
            d = self.push(a, 1, lo + h, n - h, self.s, -1)
            return [u, d]

        def first_forward(self):
            h = self.n // 2
            self.a_up.wait_recv()
            self.f_up = self.push(-1, 0, 0, h, self.f, 1)
            self.a_dn.wait_recv()
            self.f_dn = self.push(1, 0, h, self.n - h, self.f, -1)

    gp = Group("z", "x", 0, ZFIRST)
    gq = Group("x", "z", ZFIRST, NB - ZFIRST)
    last = []
    gp.first_start()
    gq.first_start()
    p0 = gp.second_start(0, 0, gp.n)
    q0 = gq.second_start(0, 0, gq.n)
    arrivals = []
    for k, dev in enumerate(other_cols(), 1):
        arrivals.append(copies.start(cot.at[pl.ds(2 * ((c + k) % NC), 2)], cotx.at[c], dev))
    keep = pltpu.make_async_copy(cot.at[pl.ds(2 * c, 2)], cotx.at[c], lsem.at[1])
    keep.start()
    wt[...] = w[...].T
    gq.first_forward()
    gp.first_forward()
    pu = gp.second_start(-1, 0, gp.n)
    pd = gp.second_start(1, 0, gp.n)
    last += gp.second_forward(p0)
    qu = gq.second_start(-1, 0, gq.n)
    qd = gq.second_start(1, 0, gq.n)
    last += gq.second_forward(q0)
    for g, pair in ((gq, []), (gp, [])):
        h = g.n // 2
        g.f_up.wait_recv()
        g.i_up = g.second_start(-2, 0, h)
        g.f_dn.wait_recv()
        g.i_dn = g.second_start(2, h, g.n - h)
    last += gp.second_forward(pu)
    last += gp.second_forward(pd)
    last += gq.second_forward(qu)
    last += gq.second_forward(qd)
    last += gq.second_forward(gq.i_up)
    last += gq.second_forward(gq.i_dn)
    last += gp.second_forward(gp.i_up)
    last += gp.second_forward(gp.i_dn)
    for cp in last + arrivals:
        cp.wait_recv()
    local.wait()
    keep.wait()
    copies.finish()


N_GATHER = 2 * (2 + 2 + 10 + 10) + NC - 1


def gather_rows(features, degree, cotangent, weight):
    vm = pl.BlockSpec(memory_space=pltpu.VMEM)
    hb = pl.BlockSpec(memory_space=pl.ANY)
    return pl.pallas_call(
        gather_kernel,
        name="gather_rows",
        out_shape=(
            jax.ShapeDtypeStruct((NR * NB, FS, BLK), BF),
            jax.ShapeDtypeStruct(weight.shape, BF),
            jax.ShapeDtypeStruct((NC, 2, FS, BLK), BF),
        ),
        in_specs=[vm, vm, hb, vm],
        out_specs=(hb, vm, hb),
        scratch_shapes=[
            pltpu.VMEM((NB, FS, BLK), BF),
            pltpu.SemaphoreType.DMA((N_GATHER,)),
            pltpu.SemaphoreType.DMA((N_GATHER,)),
            pltpu.SemaphoreType.DMA((2,)),
        ],
        compiler_params=pltpu.CompilerParams(
            collective_id=0, has_side_effects=True, vmem_limit_bytes=24 << 20
        ),
    )(features, degree, cotangent, weight)


def aggregate_kernel(col, row, count, gathered, deg, a, hidden, acc):
    step = pl.program_id(0)

    @pl.when(step == 0)
    def _():
        acc[...] = jnp.zeros_like(acc)

    @pl.when(step * TB < count[0])
    def _():
        for k in range(TB):
            t = step * TB + k
            m = lax.dot_general(
                gathered[col[t]], a[k], (((1,), (1,)), ((), ())), preferred_element_type=F32
            )
            acc[row[t]] += m

    @pl.when(step == pl.num_programs(0) - 1)
    def _():
        for b in range(NB):
            s = lax.rsqrt(deg[pl.ds(b, 1), :].astype(F32))
            hidden[b] = (acc[b] * s).astype(BF)


def last_live(i, count):
    return jnp.minimum(i, (count[0] + TB - 1) // TB - 1)


def aggregate(gathered, degree, tile_col, tile_row, tile_count, tile_weights):
    tiles = tile_col.shape[0]
    return pl.pallas_call(
        aggregate_kernel,
        name="aggregate",
        out_shape=jax.ShapeDtypeStruct((NB, FS, BLK), BF),
        grid_spec=pltpu.PrefetchScalarGridSpec(
            num_scalar_prefetch=3,
            grid=(tiles // TB,),
            in_specs=[
                pl.BlockSpec((NR * NB, FS, BLK), lambda i, *_: (0, 0, 0)),
                pl.BlockSpec((NB, BLK), lambda i, *_: (0, 0)),
                pl.BlockSpec((TB, BLK, BLK), lambda i, c, r, n: (last_live(i, n), 0, 0)),
            ],
            out_specs=pl.BlockSpec((NB, FS, BLK), lambda i, *_: (0, 0, 0)),
            scratch_shapes=[pltpu.VMEM((NB, FS, BLK), F32)],
        ),
        compiler_params=pltpu.CompilerParams(vmem_limit_bytes=32 << 20),
    )(tile_col, tile_row, tile_count, gathered, degree, tile_weights)


def dense_kernel(hid, cotx, w, wt, deg, act, back, wg, hx, act_s, back_s, send, recv, lsem):
    c = lax.axis_index("cols")
    devs = other_cols()
    greet(devs)
    copies = Copies(send, recv)
    arrivals = [
        copies.start(hid.at[pl.ds(2 * ((c + k) % NC), 2)], hx.at[c], dev)
        for k, dev in enumerate(devs, 1)
    ]
    hx[c] = hid[pl.ds(2 * c, 2)]
    for cp in arrivals:
        cp.wait_recv()

    def wide(ref):
        return jnp.concatenate([ref[:, 0].reshape(NC * FS, BLK), ref[:, 1].reshape(NC * FS, BLK)], axis=1)

    def narrow(ref, value):
        for b in range(2):
            ref[:, b] = value[:, b * BLK : (b + 1) * BLK].reshape(NC, FS, BLK)

    def spread_out(src, dst, sem):
        got = [
            copies.start(src.at[(c + k) % NC], dst.at[pl.ds(2 * c, 2)], dev)
            for k, dev in enumerate(devs, 1)
        ]
        mine = pltpu.make_async_copy(src.at[c], dst.at[pl.ds(2 * c, 2)], sem)
        mine.start()
        return got, mine

    x = wide(hx)
    pre = jnp.dot(wt[...], x, preferred_element_type=F32)
    sig = jax.nn.sigmoid(pre)
    narrow(act_s, (pre * sig).astype(BF))
    got_a, mine_a = spread_out(act_s, act, lsem.at[0])
    slope = (wide(cotx).astype(F32) * sig * (1.0 + pre * (1.0 - sig))).astype(BF)
    s = jnp.concatenate(
        [lax.rsqrt(deg[pl.ds(2 * c + b, 1), :].astype(F32)) for b in range(2)], axis=1
    )
    bk = jnp.dot(w[...], slope, preferred_element_type=F32) * s
    narrow(back_s, bk.astype(BF))
    got_b, mine_b = spread_out(back_s, back, lsem.at[1])
    wg[...] = (
        lax.dot_general(x, slope, (((1,), (1,)), ((), ())), preferred_element_type=F32)
        .astype(BF)
        .reshape(wg.shape)
    )
    for cp in got_a + got_b:
        cp.wait_recv()
    mine_a.wait()
    mine_b.wait()
    copies.finish()


def dense(hidden, cotx, weight, wt, degree):
    vm = pl.BlockSpec(memory_space=pltpu.VMEM)
    hb = pl.BlockSpec(memory_space=pl.ANY)
    n = 3 * (NC - 1)
    return pl.pallas_call(
        dense_kernel,
        name="dense",
        out_shape=(
            jax.ShapeDtypeStruct((NB, FS, BLK), BF),
            jax.ShapeDtypeStruct((NB, FS, BLK), BF),
            jax.ShapeDtypeStruct((NC, FS, weight.shape[1]), BF),
        ),
        in_specs=[vm] * 5,
        out_specs=(hb, hb, vm),
        scratch_shapes=[
            pltpu.VMEM((NC, 2, FS, BLK), BF),
            pltpu.VMEM((NC, 2, FS, BLK), BF),
            pltpu.VMEM((NC, 2, FS, BLK), BF),
            pltpu.SemaphoreType.DMA((n,)),
            pltpu.SemaphoreType.DMA((n,)),
            pltpu.SemaphoreType.DMA((2,)),
        ],
        compiler_params=pltpu.CompilerParams(
            collective_id=1, has_side_effects=True, vmem_limit_bytes=24 << 20
        ),
    )(hidden, cotx, weight, wt, degree)


def spread_kernel(col, row, count, back, a, out, acc):
    step = pl.program_id(0)

    @pl.when(step == 0)
    def _():
        out[...] = jnp.zeros_like(out)
        acc[...] = jnp.zeros_like(acc)

    @pl.when(step * TB < count[0])
    def _():
        run = acc[...]
        for k in range(TB):
            t = step * TB + k
            m = jnp.dot(back[row[t]], a[k], preferred_element_type=F32)
            same = col[t] == col[jnp.maximum(t - 1, 0)]
            run = jnp.where(same, run, 0.0) + m
            out[col[t]] = run.astype(BF)
        acc[...] = run


def spread(back, tile_col, tile_row, tile_count, tile_weights):
    tiles = tile_col.shape[0]
    return pl.pallas_call(
        spread_kernel,
        name="spread",
        out_shape=jax.ShapeDtypeStruct((NR * NB, FS, BLK), BF),
        grid_spec=pltpu.PrefetchScalarGridSpec(
            num_scalar_prefetch=3,
            grid=(tiles // TB,),
            in_specs=[
                pl.BlockSpec((NB, FS, BLK), lambda i, *_: (0, 0, 0)),
                pl.BlockSpec((TB, BLK, BLK), lambda i, c, r, n: (last_live(i, n), 0, 0)),
            ],
            out_specs=pl.BlockSpec((NR * NB, FS, BLK), lambda i, *_: (0, 0, 0)),
            scratch_shapes=[pltpu.VMEM((FS, BLK), F32)],
        ),
        compiler_params=pltpu.CompilerParams(vmem_limit_bytes=32 << 20),
    )(tile_col, tile_row, tile_count, back, tile_weights)


def scatter_kernel(
    part, deg, wg, out, wout, inner, summed, half, tail, wy, ws, wc, wm, wz, w1, wx, w2, wv, send, recv
):
    c = lax.axis_index("cols")
    y, low = c // 4, c % 4
    zl, core = low // 2, low % 2
    ypeers = [{"cols": ((y + k) % NY) * 4 + low} for k in range(1, NY)]
    cpeer = {"cols": c + 1 - 2 * core}
    zpeer = {"cols": c + 2 - 4 * zl}
    xs = [{"rows": rank_along("x", k)} for k in range(1, NX)]
    zs = [{"rows": rank_along("z", k)} for k in range(1, NZ)]
    greet(ypeers + [cpeer, zpeer] + xs + zs)
    copies = Copies(send, recv)

    class Group:
        def __init__(self, first, second, lo, n):
            self.f, self.s, self.lo, self.n = first, second, lo, n

        def local(self, a, b):
            return part.at[pl.ds(owner_at(self.f, a, self.s, b) * NB + self.lo, self.n)]

    def ring_start(axis, n, shard, land):
        h = n // 2
        up, dn = {"rows": rank_along(axis, 1)}, {"rows": rank_along(axis, -1)}
        return {
            "n": n,
            "up": up,
            "dn": dn,
            "shard": shard,
            "land": land,
            "far_dn": copies.start(shard(-2).at[pl.ds(0, h)], land.at[pl.ds(0, h)], dn),
            "far_up": copies.start(shard(2).at[pl.ds(h, n - h)], land.at[pl.ds(h, n - h)], up),
            "raw_dn": copies.start(shard(-1).at[pl.ds(h, n - h)], land.at[pl.ds(n + h, n - h)], dn),
            "raw_up": copies.start(shard(1).at[pl.ds(0, h)], land.at[pl.ds(2 * n, h)], up),
        }

    def add_into(dst, a, b):
        def one(i, carry):
            dst[i] = (a[i].astype(F32) + b[i].astype(F32)).astype(BF)
            return carry

        lax.fori_loop(0, dst.shape[0], one, 0, unroll=2)

    def ring_forward(r, work):
        n, land = r["n"], r["land"]
        h = n // 2
        r["far_dn"].wait_recv()
        add_into(work.at[pl.ds(0, h)], land.at[pl.ds(0, h)], r["shard"](-1).at[pl.ds(0, h)])
        r["sum_dn"] = copies.start(work.at[pl.ds(0, h)], land.at[pl.ds(n, h)], r["dn"])
        r["far_up"].wait_recv()
        add_into(
            work.at[pl.ds(h, n - h)], land.at[pl.ds(h, n - h)], r["shard"](1).at[pl.ds(h, n - h)]
        )
        r["sum_up"] = copies.start(work.at[pl.ds(h, n - h)], land.at[pl.ds(2 * n + h, n - h)], r["up"])

    def ring_end(r, store):
        n, land = r["n"], r["land"]
        for name in ("raw_dn", "raw_up", "sum_dn", "sum_up"):
            r[name].wait_recv()
        mine = r["shard"](0)

        def one(i, carry):
            store(i, mine[i].astype(F32) + land[n + i].astype(F32) + land[2 * n + i].astype(F32))
            return carry

        lax.fori_loop(0, n, one, 0, unroll=2)

    order = (2, -1, 1, 0)
    gp = Group("x", "z", 0, ZFIRST)
    gq = Group("z", "x", ZFIRST, NB - ZFIRST)
    rings = {}
    for i, b in enumerate(order):
        for g in (gp, gq):
            shard = lambda a, g=g, b=b: g.local(a, b)
            land = inner.at[i, pl.ds(3 * g.lo, 3 * g.n)]
            rings[g, b] = ring_start(g.f, g.n, shard, land)
    wys = [
        copies.start(wg.at[pl.ds(4 * ((y + k) % NY), 4)], wy.at[k - 1], d)
        for k, d in enumerate(ypeers, 1)
    ]

    def keep(g, i):
        def store(j, v):
            summed[i, g.lo + j] = v.astype(BF)

        return store

    for i, b in enumerate(order):
        for g in (gp, gq):
            ring_forward(rings[g, b], half.at[i, pl.ds(g.lo, g.n)])
        if i == 1:
            for cp in wys:
                cp.wait_recv()
            for j in range(4):
                v = wg[4 * y + j].astype(F32)
                for k in range(NY - 1):
                    v = v + wy[k, j].astype(F32)
                ws[j] = v.astype(BF)
            wcs = [copies.start(ws.at[2 * q + 1 - core], wc.at[q], cpeer) for q in range(2)]
    second = {}
    for i, b in enumerate(order):
        for g in (gp, gq):
            ring_end(rings[g, b], keep(g, i))
    for cp in wcs:
        cp.wait_recv()
    for q in range(2):
        wm[q] = (ws[2 * q + core].astype(F32) + wc[q].astype(F32)).astype(BF)
    wzc = copies.start(wm.at[1 - zl], wz, zpeer)
    place = {2: 0, -2: 0, -1: 1, 1: 2, 0: 3}
    for g in (gp, gq):
        shard = lambda a, g=g: summed.at[place[a], pl.ds(g.lo, g.n)]
        second[g] = ring_start(g.s, g.n, shard, tail.at[pl.ds(3 * g.lo, 3 * g.n)])
    wzc.wait_recv()
    w1[...] = (wm[zl].astype(F32) + wz[...].astype(F32)).astype(BF)
    wxs = [copies.start(w1, wx.at[k], d) for k, d in enumerate(xs)]
    for g in (gp, gq):
        ring_forward(second[g], half.at[4, pl.ds(g.lo, g.n)])
    for cp in wxs:
        cp.wait_recv()
    v = w1[...].astype(F32)
    for k in range(NX - 1):
        v = v + wx[k].astype(F32)
    w2[...] = v.astype(BF)
    wvs = [copies.start(w2, wv.at[k], d) for k, d in enumerate(zs)]
    for g in (gp, gq):

        def final(j, v, g=g):
            s = lax.rsqrt(deg[pl.ds(g.lo + j, 1), :].astype(F32))
            out[g.lo + j] = (v * s).astype(BF)

        ring_end(second[g], final)
    for cp in wvs:
        cp.wait_recv()
    v = w2[...].astype(F32)
    for k in range(NZ - 1):
        v = v + wv[k].astype(F32)
    wout[...] = v
    copies.finish()


N_SCATTER = 2 * (4 * 6 + 6) + (NY - 1) + 2 + 1 + (NX - 1) + (NZ - 1)


def scatter_rows(part, degree, wg):
    vm = pl.BlockSpec(memory_space=pltpu.VMEM)
    f = wg.shape[2]
    return pl.pallas_call(
        scatter_kernel,
        name="scatter_rows",
        out_shape=(
            jax.ShapeDtypeStruct((NB, FS, BLK), BF),
            jax.ShapeDtypeStruct((FS, f), F32),
        ),
        in_specs=[vm] * 3,
        out_specs=(vm, vm),
        scratch_shapes=[
            pltpu.VMEM((4, 3 * NB, FS, BLK), BF),
            pltpu.VMEM((4, NB, FS, BLK), BF),
            pltpu.VMEM((5, NB, FS, BLK), BF),
            pltpu.VMEM((3 * NB, FS, BLK), BF),
            pltpu.VMEM((NY - 1, 4, FS, f), BF),
            pltpu.VMEM((4, FS, f), BF),
            pltpu.VMEM((2, FS, f), BF),
            pltpu.VMEM((2, FS, f), BF),
            pltpu.VMEM((FS, f), BF),
            pltpu.VMEM((FS, f), BF),
            pltpu.VMEM((NX - 1, FS, f), BF),
            pltpu.VMEM((FS, f), BF),
            pltpu.VMEM((NZ - 1, FS, f), BF),
            pltpu.SemaphoreType.DMA((N_SCATTER,)),
            pltpu.SemaphoreType.DMA((N_SCATTER,)),
        ],
        compiler_params=pltpu.CompilerParams(
            collective_id=2, has_side_effects=True, vmem_limit_bytes=32 << 20
        ),
    )(part, degree, wg)


def body(features, cotangent, weight, degree, tile_row, tile_col, tile_count, tile_weights):
    gathered, wt, cotx = gather_rows(features, degree, cotangent, weight)
    hidden = aggregate(gathered, degree, tile_col, tile_row, tile_count, tile_weights)
    activated, back, wg = dense(hidden, cotx, weight, wt, degree)
    part = spread(back, tile_col, tile_row, tile_count, tile_weights)
    input_grad, weight_grad = scatter_rows(part, degree, wg)
    return (activated, input_grad, weight_grad)


def solution(mesh):
    in_specs = (
        P("rows", "cols", None),
        P("rows", "cols", None),
        P(),
        P("rows", None),
        P("rows"),
        P("rows"),
        P("rows"),
        P("rows", None, None),
    )
    out_specs = (P("rows", "cols", None), P("rows", "cols", None), P("cols", None))
    return jax.shard_map(body, mesh=mesh, in_specs=in_specs, out_specs=out_specs, check_vma=False)
```

time: 389 us -> 141 us (0.36); the launches traced: 385 us -> 141 us
  waiting for transfers between devices: 185 us -> 0 us
  Pallas kernels: 0 us -> 128 us
  other arithmetic: 68.7 us -> 0 us
  blocking collectives: 66.1 us -> 0 us
  matrix products: 31 us -> 0 us
  between operations: 14.5 us -> 1.39 us
  local copies, waits for them, and re-layouts: 19.3 us -> 11.2 us
    all_gather x3 -> x0, waiting for transfers between devices: 159 us -> none  [the longest x1 80.3 us: body(): gathered = lax.all_gather(scaled, 'rows', axis=0, tiled=True)]
    pallas_call x0 -> x5, Pallas kernels: none -> 128 us  [the longest x1 57.2 us: scatter_rows(): pl.pallas_call(scatter_kernel, name='scatter_rows', out_shape=(jax.ShapeD...]
    psum x1 -> x0, blocking collectives: 66.1 us -> none  [body(): lax.psum(grad_rows.astype(jnp.bfloat16), 'rows').astype(jnp.float32)]
    scatter-add x8 -> x0, other arithmetic: 44.9 us -> none  [the longest x4 32.2 us: spread_advance(): return current.at[local_ids].add(contrib)]
    dot_general x11 -> x0, matrix products: 31 us -> none  [the longest x4 11.3 us: aggregate_advance(): jnp.einsum('tfj,tij->tfi', blocks, adjacency, preferred_element_type=jnp....]
    reduce_scatter x1 -> x0, waiting for transfers between devices: 25.7 us -> none  [body(): lax.psum_scatter(partial_value.astype(jnp.bfloat16), 'rows', scatter_dime...]
    gather x8 -> x0, local copies, waits for them, and re-layouts: 14 us -> none  [the longest x4 11.4 us: aggregate_advance(): blocks = jnp.take(source, local_ids, axis=0)]
    convert_element_type x5 -> x0, other arithmetic: 11.1 us -> none  [the longest x1 6.34 us: body(): partial_value.astype(jnp.bfloat16)]
  transfers between devices with their start and end apart: 4 -> 0, of which waited for: 4 -> 0; matrix products, arithmetic and copies ran while one was open for 1% -> 0% of each run, Pallas kernels for 0% -> 0%
where the time goes in v1:
time: 141 us
  Pallas kernels  128 us (91%)
  local copies, waits for them, and re-layouts  11.2 us (8%)
    pallas_call x1, Pallas kernels, scatter_rows(): pl.pallas_call(scatter_kernel, name='scatter_rows', out_shape=(jax.ShapeD...  57.2 us
    pallas_call x1, Pallas kernels, gather_rows(): pl.pallas_call(gather_kernel, name='gather_rows', out_shape=(jax.ShapeDty...  44.7 us
    pallas_call x1, Pallas kernels, dense(): pl.pallas_call(dense_kernel, name='dense', out_shape=(jax.ShapeDtypeStruc...  21.3 us
    unnamed x29, local copies, waits for them, and re-layouts  11.2 us

profile of v1, /device:TPU:33, one launch (start us, length us, event | category | flops | bytes accessed | tf_op | source)
XLA Modules:
  0.0 141.0 jit_solution(2581671320515115179)
XLA Ops:
  1.3 0.0 copy-start.2
  1.3 1.0 copy-done.2
  2.3 0.0 copy-start.4
  2.3 0.7 copy-done.4
  3.0 0.0 copy-start.7
  3.0 0.9 copy-done.7
  4.0 0.0 copy-start.8
  4.0 0.9 copy-done.8
  4.9 44.7 %gather_rows.1 = (bf16[512,32,128]{2,1,0:T(8,128)(2,1)S(1)}, bf16[512,512]{1,0:T(8,128)(2,1)S(1)}, bf16[16,2,32,128]{3,2,1,0:T(8,128)(2,1)S(1)}) custom-call(bf16[32,32,128]{2,1,0:T(8,128)(2,1)S(1)} %copy-done.7, s32[32,128]{1,0:T(8,128)S(1)} %copy-done.4, bf16[32,32,128]{2,1,0:T(8,128)(2,1)S(1)} %copy-done.8, bf16[512,512]{1,0:T(8,128)(2,1)S(1)} %copy-done.2), custom_call_target="tpu_custom_call" | custom-call | tf_op jit(solution)/shard_map/gather_rows/pallas_call | solution.py:173
  49.6 0.0 copy-start
  49.6 3.4 %copy-done = bf16[256,128,128]{2,1,0:T(8,128)(2,1)S(1)} copy-done((bf16[256,128,128]{2,1,0:T(8,128)(2,1)S(1)}, bf16[256,128,128]{2,1,0:T(8,128)(2,1)}, u32[]{:S(2)}) %copy-start) | copy-done | bytes 8388632
  53.0 0.0 copy-start.5
  53.0 0.7 copy-done.5
  53.7 0.0 copy-start.9
  53.7 0.7 copy-done.9
  54.4 0.0 copy-start.11
  54.4 0.7 copy-done.11
  55.1 0.0 copy-start.3
  55.1 0.0 copy-start.1
  55.1 0.0 copy-start.10
  55.1 0.0 copy-start.12
  55.1 2.7 %aggregate.1.hid = bf16[32,32,128]{2,1,0:T(8,128)(2,1)S(1)} custom-call(s32[256]{0:T(256)S(1)} %copy-done.9, s32[256]{0:T(256)S(1)} %copy-done.11, s32[1]{0:T(128)S(6)} %copy.14.count, bf16[512,32,128]{2,1,0:T(8,128)(2,1)S(1)} %get-tuple-element.11.gathered, s32[32,128]{1,0:T(8,128)S(1)} %copy-done.5, bf16[256,128,128]{2,1,0:T(8,128)(2,1)S(1)} %copy-done), custom_call_target="tpu_custom_call" | custom-call | tf_op jit(solution)/shard_map/aggregate/pallas_call | solution.py:224
  57.8 0.0 copy-done.3
  57.8 21.3 %dense.1 = (bf16[32,32,128]{2,1,0:T(8,128)(2,1)S(1)}, bf16[32,32,128]{2,1,0:T(8,128)(2,1)S(1)}, bf16[16,32,512]{2,1,0:T(8,128)(2,1)S(1)}) custom-call(bf16[32,32,128]{2,1,0:T(8,128)(2,1)S(1)} %aggregate.1.hid, bf16[16,2,32,128]{3,2,1,0:T(8,128)(2,1)S(1)} %get-tuple-element.12.cotx, bf16[512,512]{1,0:T(8,128)(2,1)S(1)} %copy-done.3, ...), custom_call_target="tpu_custom_call" | custom-call | tf_op jit(solution)/shard_map/dense/pallas_call | solution.py:300
  79.1 0.0 copy-done.1
  79.1 0.0 copy-done.10
  79.1 0.0 copy-done.12
  79.1 0.0 copy-start.6
  79.1 2.6 %spread.1.part = bf16[512,32,128]{2,1,0:T(8,128)(2,1)S(1)} custom-call(s32[256]{0:T(256)S(1)} %copy-done.10, s32[256]{0:T(256)S(1)} %copy-done.12, s32[1]{0:T(128)S(6)} %copy.14.count, bf16[32,32,128]{2,1,0:T(8,128)(2,1)S(1)} %get-tuple-element.15.back, bf16[256,128,128]{2,1,0:T(8,128)(2,1)S(1)} %copy-done.1), custom_call_target="tpu_custom_call" | custom-call | tf_op jit(solution)/shard_map/spread/pallas_call | solution.py:346
  81.8 0.0 copy-done.6
  81.8 57.2 %scatter_rows.1 = (bf16[32,32,128]{2,1,0:T(8,128)(2,1)S(1)}, f32[32,512]{1,0:T(8,128)S(1)}) custom-call(bf16[512,32,128]{2,1,0:T(8,128)(2,1)S(1)} %spread.1.part, s32[32,128]{1,0:T(8,128)S(1)} %copy-done.6, bf16[16,32,512]{2,1,0:T(8,128)(2,1)S(1)} %get-tuple-element.16.wg), custom_call_target="tpu_custom_call" | custom-call | tf_op jit(solution)/shard_map/scatter_rows/pallas_call | solution.py:510
  138.9 0.7 copy.15
  139.6 0.7 copy.16
  140.3 0.6 copy.17
Async XLA Ops:
  1.3 1.0 copy-start.2
  2.3 0.7 copy-start.4
  3.0 0.9 copy-start.7
  4.0 0.9 copy-start.8
  49.6 3.4 %copy-start = (bf16[256,128,128]{2,1,0:T(8,128)(2,1)S(1)}, bf16[256,128,128]{2,1,0:T(8,128)(2,1)}, u32[]{:S(2)}) copy-start(bf16[256,128,128]{2,1,0:T(8,128)(2,1)} %a.3) | copy-start | bytes 25165828
  53.0 0.7 copy-start.5
  53.7 0.7 copy-start.9
  54.4 0.7 copy-start.11
  55.1 2.7 %copy-start.3 = (bf16[512,512]{1,0:T(8,128)(2,1)S(1)}, bf16[512,512]{1,0:T(8,128)(2,1)}, u32[]{:S(2)}) copy-start(bf16[512,512]{1,0:T(8,128)(2,1)} %w.3) | copy-start | bytes 1572868
  55.1 24.0 %copy-start.1 = (bf16[256,128,128]{2,1,0:T(8,128)(2,1)S(1)}, bf16[256,128,128]{2,1,0:T(8,128)(2,1)}, u32[]{:S(2)}) copy-start(bf16[256,128,128]{2,1,0:T(8,128)(2,1)} %a.3) | copy-start | bytes 25165828
  55.1 24.0 %copy-start.10 = (s32[256]{0:T(256)S(1)}, s32[256]{0:T(256)}, u32[]{:S(2)}) copy-start(s32[256]{0:T(256)} %col.3) | copy-start | bytes 3076
  55.1 24.0 %copy-start.12 = (s32[256]{0:T(256)S(1)}, s32[256]{0:T(256)}, u32[]{:S(2)}) copy-start(s32[256]{0:T(256)} %row.3) | copy-start | bytes 3076
  79.1 2.6 %copy-start.6 = (s32[32,128]{1,0:T(8,128)S(1)}, s32[32,128]{1,0:T(8,128)}, u32[]{:S(2)}) copy-start(s32[32,128]{1,0:T(8,128)} %deg.7) | copy-start | bytes 49156

commit v2 on v1

v2 whole, which is shorter than its diff:
```python
import functools

import jax
import jax.numpy as jnp
from jax import lax
from jax.experimental import pallas as pl
from jax.experimental.pallas import tpu as pltpu
from jax.sharding import PartitionSpec as P

BF = jnp.bfloat16
F32 = jnp.float32
NB = 32
FS = 32
BLK = 128
NX = 4
NZ = 4
NR = NX * NZ
NY = 4
NC = 16
ZFIRST = 26
TB = 16
T = 256
DEAD = 1024


def rank_along(axis, step):
    r = lax.axis_index("rows")
    x, z = r // NZ, r % NZ
    if axis == "x":
        return ((x + step + NX) % NX) * NZ + z
    return x * NZ + (z + step + NZ) % NZ


def owner_at(first, a, second, b):
    r = lax.axis_index("rows")
    step = {first: a, second: b}
    return ((r // NZ + step["x"] + NX) % NX) * NZ + (r % NZ + step["z"] + NZ) % NZ


class Copies:
    def __init__(self, send, recv):
        self.send, self.recv, self.n, self.started = send, recv, 0, []

    def start(self, src, dst, device):
        k = self.n
        self.n += 1
        c = pltpu.make_async_remote_copy(
            src_ref=src,
            dst_ref=dst,
            send_sem=self.send.at[k],
            recv_sem=self.recv.at[k],
            device_id=device,
            device_id_type=pl.DeviceIdType.MESH,
        )
        c.start()
        self.started.append(c)
        return c

    def finish(self):
        for c in self.started:
            c.wait_send()


def greet(devices):
    barrier = pltpu.get_barrier_semaphore()
    for d in devices:
        pl.semaphore_signal(barrier, inc=1, device_id=d, device_id_type=pl.DeviceIdType.MESH)


def greeted(devices):
    pl.semaphore_wait(pltpu.get_barrier_semaphore(), len(devices))


def other_cols():
    c = lax.axis_index("cols")
    return [{"cols": (c + k) % NC} for k in range(1, NC)]


PERM, COLP, KEYP, ROW, COL, COLEND, ROWEND = range(7)


def tile_order(rowcol, count, idx_v):
    i32 = jnp.int32
    lane = lax.broadcasted_iota(i32, (1, T), 1)
    live = lane < count[0]
    row, col = rowcol[0], rowcol[1]
    key = jnp.where(live, row, DEAD)
    ckey = jnp.where(live, col, DEAD)

    def down(v):
        return jnp.broadcast_to(v, (8, T)).T[:, :1]

    def total(mask):
        return jnp.sum(mask.astype(i32), axis=0, keepdims=True)

    key_d, col_d, ckey_d = down(key), down(col), down(ckey)
    sub = lax.broadcasted_iota(i32, (T, T), 0)
    across = lax.broadcasted_iota(i32, (T, T), 1)
    pos = total((key_d < key) | ((key_d == key) & (sub < across)))
    here = down(pos) == across

    def sorted_(v_d):
        return jnp.sum(jnp.where(here, v_d, 0), axis=0, keepdims=True)

    def ends(v_d, n):
        b = lax.broadcasted_iota(i32, (T, n), 1)
        return jnp.where(total(v_d == b) > 0, total(v_d <= b) - 1, T)

    idx_v[pl.ds(PERM, 1), :T] = sorted_(sub)
    idx_v[pl.ds(COLP, 1), :T] = sorted_(col_d)
    idx_v[pl.ds(KEYP, 1), :T] = sorted_(key_d)
    idx_v[pl.ds(ROW, 1), :T] = row
    idx_v[pl.ds(COL, 1), :T] = ckey
    idx_v[pl.ds(COLEND, 1), :] = ends(ckey_d, NR * NB)
    idx_v[pl.ds(ROWEND, 1), :BLK] = ends(key_d, BLK)


def layer_kernel(
    feat, cot, w_h, deg_h, row_h, col_h, count, a_h,
    act, out, wout,
    fbuf, deg, w, wt, rowcol, a, idx_v, idx, gat, cotx, sums, hid, hx, act_s, back_s, back, runs, part, wg,
    inner, summed, half, tail, wy, ws, wc, wm, wz, w1, wx, w2, wv,
    send, recv, lsem,
):
    me = lax.axis_index("rows")
    c = lax.axis_index("cols")
    y, low = c // 4, c % 4
    zl, core = low // 2, low % 2
    devs = other_cols()
    ypeers = [{"cols": ((y + k) % NY) * 4 + low} for k in range(1, NY)]
    cpeer = {"cols": c + 1 - 2 * core}
    zpeer = {"cols": c + 2 - 4 * zl}
    xs = [{"rows": rank_along("x", k)} for k in range(1, NX)]
    zs = [{"rows": rank_along("z", k)} for k in range(1, NZ)]
    peers = devs + xs + zs
    greet(peers)
    loads = []

    def load(src, dst):
        cp = pltpu.make_async_copy(src, dst, lsem.at[len(loads)])
        cp.start()
        loads.append(cp)
        return cp

    l_feat = load(feat, fbuf)
    l_deg = load(deg_h, deg)
    l_idx = [load(row_h, rowcol.at[0]), load(col_h, rowcol.at[1])]
    l_w = load(w_h, w)
    l_cot = load(cot.at[pl.ds(2 * c, 2)], cotx.at[c])
    l_a = [load(a_h.at[pl.ds(i * T // 4, T // 4)], a.at[pl.ds(i * T // 4, T // 4)]) for i in range(4)]
    l_feat.wait()
    l_deg.wait()

    def scale_of(b):
        return lax.rsqrt(deg[pl.ds(b, 1), :].astype(F32))

    def scale_block(b, carry):
        gat[me * NB + b] = (fbuf[b].astype(F32) * scale_of(b)).astype(BF)
        return carry

    lax.fori_loop(0, NB, scale_block, 0, unroll=4)
    greeted(peers)
    copies = Copies(send, recv)

    class Gather:
        def __init__(self, first, second, lo, n, chunks):
            self.f, self.s, self.chunks = first, second, chunks
            self.size = n // chunks
            self.at = [lo + i * self.size for i in range(chunks)]
            h = chunks // 2
            self.up_order = list(range(chunks))
            self.dn_order = list(range(chunks))[::-1]
            self.up_half = self.up_order[:h]
            self.dn_half = self.dn_order[: chunks - h]
            self.a, self.b = {}, {}

        def push(self, a, b, i, axis, step):
            at = self.at[i]
            ds = pl.ds(owner_at(self.f, a, self.s, b) * NB + at, self.size)
            return copies.start(gat.at[ds], gat.at[ds], {"rows": rank_along(axis, step)})

        def first_start(self):
            for u, d in zip(self.up_order, self.dn_order):
                self.a[-1, u] = self.push(0, 0, u, self.f, 1)
                self.a[1, d] = self.push(0, 0, d, self.f, -1)

        def first_forward(self, j, then=None):
            for side, order, half in ((-1, self.up_order, self.up_half), (1, self.dn_order, self.dn_half)):
                i = order[j]
                self.a[side, i].wait_recv()
                if i in half:
                    self.a[2 * side, i] = self.push(side, 0, i, self.f, -side)
                if then:
                    then(side, i)

        def far(self, j, then):
            for side, half in ((-1, self.up_half), (1, self.dn_half)):
                if j < len(half):
                    self.a[2 * side, half[j]].wait_recv()
                    then(2 * side, half[j])

        def second_start(self, a, i):
            self.b[a, -1, i] = self.push(a, 0, i, self.s, 1)
            self.b[a, 1, i] = self.push(a, 0, i, self.s, -1)

        def second_forward(self, a, i):
            side = -1 if i in self.up_half else 1
            self.b[a, side, i].wait_recv()
            last.append(self.push(a, side, i, self.s, -side))
            last.append(self.b[a, -side, i])

    PC, QC = 2, 2
    last = []
    gp = Gather("z", "x", 0, ZFIRST, PC)
    gq = Gather("x", "z", ZFIRST, NB - ZFIRST, QC)
    gp.first_start()
    gq.first_start()
    for i in range(PC):
        gp.second_start(0, i)
    for k, dev in enumerate(devs, 1):
        last.append(copies.start(cot.at[pl.ds(2 * ((c + k) % NC), 2)], cotx.at[c], dev))
    for cp in l_idx:
        cp.wait()
    tile_order(rowcol, count, idx_v)
    l_s = load(idx_v, idx)
    l_w.wait()
    wt[...] = w[...].T
    for j in range(QC):
        gq.first_forward(j)
    for j in range(PC):
        gp.first_forward(j, gp.second_start)
    for i in range(QC):
        gq.second_start(0, i)
    for i in range(PC):
        gp.second_forward(0, i)
    for j in range(QC):
        gq.second_start(-1, gq.up_order[j])
        gq.second_start(1, gq.dn_order[j])
    for j in range((PC + 1) // 2):
        gp.far(j, gp.second_start)
    for i in range(PC):
        gp.second_forward(-1, i)
        gp.second_forward(1, PC - 1 - i)
    for i in range(QC):
        gq.second_forward(0, i)
    for j in range((QC + 1) // 2):
        gq.far(j, gq.second_start)
    for i in range(QC):
        gq.second_forward(-1, i)
        gq.second_forward(1, QC - 1 - i)
    for j in range((PC + 1) // 2):
        gp.second_forward(-2, gp.up_half[j])
        gp.second_forward(2, gp.dn_half[j])
    for j in range((QC + 1) // 2):
        gq.second_forward(-2, gq.up_half[j])
        gq.second_forward(2, gq.dn_half[j])
    for cp in last:
        cp.wait_recv()
    for cp in l_a + [l_s, l_cot]:
        cp.wait()

    sums[T] = jnp.zeros((FS, BLK), F32)

    def forward(i, run):
        for k in range(TB):
            p = i * TB + k
            m = lax.dot_general(
                gat[idx[COLP, p]], a[idx[PERM, p]], (((1,), (1,)), ((), ())), preferred_element_type=F32
            )
            same = idx[KEYP, p] == idx[KEYP, jnp.maximum(p - 1, 0)]
            run = jnp.where(same, run, 0.0) + m
            sums[p] = run
        return run

    lax.fori_loop(0, T // TB, forward, jnp.zeros((FS, BLK), F32))

    def finish_row(b, carry):
        hid[b] = (sums[idx[ROWEND, b]] * scale_of(b)).astype(BF)
        return carry

    lax.fori_loop(0, NB, finish_row, 0, unroll=4)

    arrivals = [
        copies.start(hid.at[pl.ds(2 * ((c + k) % NC), 2)], hx.at[c], dev)
        for k, dev in enumerate(devs, 1)
    ]
    hx[c] = hid[pl.ds(2 * c, 2)]
    runs[T] = jnp.zeros((FS, BLK), BF)
    for cp in arrivals:
        cp.wait_recv()

    def wide(ref):
        return jnp.concatenate([ref[:, b].reshape(NC * FS, BLK) for b in range(2)], axis=1)

    def narrow(ref, value):
        for b in range(2):
            ref[:, b] = value[:, b * BLK : (b + 1) * BLK].reshape(NC, FS, BLK)

    def to_owner(src, dst):
        got = [
            copies.start(src.at[(c + k) % NC], dst.at[pl.ds(2 * c, 2)], dev)
            for k, dev in enumerate(devs, 1)
        ]
        return got, load(src.at[c], dst.at[pl.ds(2 * c, 2)])

    x = wide(hx)
    pre = jnp.dot(wt[...], x, preferred_element_type=F32)
    sig = jax.nn.sigmoid(pre)
    slope = (wide(cotx).astype(F32) * sig * (1.0 + pre * (1.0 - sig))).astype(BF)
    s = jnp.concatenate([scale_of(2 * c + b) for b in range(2)], axis=1)
    narrow(back_s, (jnp.dot(w[...], slope, preferred_element_type=F32) * s).astype(BF))
    got_b, mine_b = to_owner(back_s, back)
    narrow(act_s, (pre * sig).astype(BF))
    got_a, mine_a = to_owner(act_s, act)
    wg[...] = (
        lax.dot_general(x, slope, (((1,), (1,)), ((), ())), preferred_element_type=F32)
        .astype(BF)
        .reshape(wg.shape)
    )
    wys = [
        copies.start(wg.at[pl.ds(4 * ((y + k) % NY), 4)], wy.at[k - 1], d)
        for k, d in enumerate(ypeers, 1)
    ]
    for cp in got_b:
        cp.wait_recv()
    mine_b.wait()

    def backward(i, run):
        for k in range(TB):
            t = i * TB + k
            m = jnp.dot(back[idx[ROW, t]], a[t], preferred_element_type=F32)
            same = idx[COL, t] == idx[COL, jnp.maximum(t - 1, 0)]
            run = jnp.where(same, run, 0.0) + m
            runs[t] = run.astype(BF)
        return run

    lax.fori_loop(0, T // TB, backward, jnp.zeros((FS, BLK), F32))

    def pick(i, carry):
        part[i] = runs[idx[COLEND, i]]
        return carry

    lax.fori_loop(0, NR * NB, pick, 0, unroll=8)

    class Shards:
        def __init__(self, first, second, lo, n):
            self.f, self.s, self.lo, self.n = first, second, lo, n

        def local(self, a, b):
            return part.at[pl.ds(owner_at(self.f, a, self.s, b) * NB + self.lo, self.n)]

    def ring_start(axis, n, shard, land):
        h = n // 2
        up, dn = {"rows": rank_along(axis, 1)}, {"rows": rank_along(axis, -1)}
        return {
            "n": n,
            "up": up,
            "dn": dn,
            "shard": shard,
            "land": land,
            "far_dn": copies.start(shard(-2).at[pl.ds(0, h)], land.at[pl.ds(0, h)], dn),
            "far_up": copies.start(shard(2).at[pl.ds(h, n - h)], land.at[pl.ds(h, n - h)], up),
            "raw_dn": copies.start(shard(-1).at[pl.ds(h, n - h)], land.at[pl.ds(n + h, n - h)], dn),
            "raw_up": copies.start(shard(1).at[pl.ds(0, h)], land.at[pl.ds(2 * n, h)], up),
        }

    def add_into(dst, a, b):
        def one(i, carry):
            dst[i] = (a[i].astype(F32) + b[i].astype(F32)).astype(BF)
            return carry

        lax.fori_loop(0, dst.shape[0], one, 0, unroll=2)

    def ring_forward(r, work):
        n, land = r["n"], r["land"]
        h = n // 2
        r["far_dn"].wait_recv()
        add_into(work.at[pl.ds(0, h)], land.at[pl.ds(0, h)], r["shard"](-1).at[pl.ds(0, h)])
        r["sum_dn"] = copies.start(work.at[pl.ds(0, h)], land.at[pl.ds(n, h)], r["dn"])
        r["far_up"].wait_recv()
        add_into(
            work.at[pl.ds(h, n - h)], land.at[pl.ds(h, n - h)], r["shard"](1).at[pl.ds(h, n - h)]
        )
        r["sum_up"] = copies.start(work.at[pl.ds(h, n - h)], land.at[pl.ds(2 * n + h, n - h)], r["up"])

    def ring_end(r, store):
        n, land = r["n"], r["land"]
        for name in ("raw_dn", "raw_up", "sum_dn", "sum_up"):
            r[name].wait_recv()
        mine = r["shard"](0)

        def one(i, carry):
            store(i, mine[i].astype(F32) + land[n + i].astype(F32) + land[2 * n + i].astype(F32))
            return carry

        lax.fori_loop(0, n, one, 0, unroll=2)

    order = (2, -1, 1, 0)
    gp = Shards("x", "z", 0, ZFIRST)
    gq = Shards("z", "x", ZFIRST, NB - ZFIRST)
    rings = {}
    for i, b in enumerate(order):
        for g in (gp, gq):
            shard = lambda a, g=g, b=b: g.local(a, b)
            land = inner.at[i, pl.ds(3 * g.lo, 3 * g.n)]
            rings[g, b] = ring_start(g.f, g.n, shard, land)

    def keep(g, i):
        def store(j, v):
            summed[i, g.lo + j] = v.astype(BF)

        return store

    for i, b in enumerate(order):
        for g in (gp, gq):
            ring_forward(rings[g, b], half.at[i, pl.ds(g.lo, g.n)])
        if i == 1:
            for cp in wys:
                cp.wait_recv()
            for j in range(4):
                v = wg[4 * y + j].astype(F32)
                for k in range(NY - 1):
                    v = v + wy[k, j].astype(F32)
                ws[j] = v.astype(BF)
            wcs = [copies.start(ws.at[2 * q + 1 - core], wc.at[q], cpeer) for q in range(2)]
    second = {}
    for i, b in enumerate(order):
        for g in (gp, gq):
            ring_end(rings[g, b], keep(g, i))
    for cp in wcs:
        cp.wait_recv()
    for q in range(2):
        wm[q] = (ws[2 * q + core].astype(F32) + wc[q].astype(F32)).astype(BF)
    wzc = copies.start(wm.at[1 - zl], wz, zpeer)
    place = {2: 0, -2: 0, -1: 1, 1: 2, 0: 3}
    for g in (gp, gq):
        shard = lambda a, g=g: summed.at[place[a], pl.ds(g.lo, g.n)]
        second[g] = ring_start(g.s, g.n, shard, tail.at[pl.ds(3 * g.lo, 3 * g.n)])
    wzc.wait_recv()
    w1[...] = (wm[zl].astype(F32) + wz[...].astype(F32)).astype(BF)
    wxs = [copies.start(w1, wx.at[k], d) for k, d in enumerate(xs)]
    for g in (gp, gq):
        ring_forward(second[g], half.at[4, pl.ds(g.lo, g.n)])
    for cp in wxs:
        cp.wait_recv()
    v = w1[...].astype(F32)
    for k in range(NX - 1):
        v = v + wx[k].astype(F32)
    w2[...] = v.astype(BF)
    wvs = [copies.start(w2, wv.at[k], d) for k, d in enumerate(zs)]
    for g in (gp, gq):

        def final(j, v, g=g):
            out[g.lo + j] = (v * scale_of(g.lo + j)).astype(BF)

        ring_end(second[g], final)
    for cp in wvs:
        cp.wait_recv()
    v = w2[...].astype(F32)
    for k in range(NZ - 1):
        v = v + wv[k].astype(F32)
    wout[...] = v
    for cp in got_a:
        cp.wait_recv()
    mine_a.wait()
    copies.finish()


N_COPIES = 2 * 2 * 15 + 4 * (NC - 1) + 2 * (4 * 6 + 6) + (NY - 1) + 2 + 1 + (NX - 1) + (NZ - 1)


def body(features, cotangent, weight, degree, tile_row, tile_col, tile_count, tile_weights):
    hb = pl.BlockSpec(memory_space=pl.ANY)
    vm = pl.BlockSpec(memory_space=pltpu.VMEM)
    sm = pl.BlockSpec(memory_space=pltpu.SMEM)
    f = weight.shape[1]
    shard = (FS, BLK)
    return pl.pallas_call(
        layer_kernel,
        name="layer",
        out_shape=(
            jax.ShapeDtypeStruct((NB,) + shard, BF),
            jax.ShapeDtypeStruct((NB,) + shard, BF),
            jax.ShapeDtypeStruct((FS, f), F32),
        ),
        in_specs=[hb, hb, hb, hb, hb, hb, sm, hb],
        out_specs=(hb, vm, vm),
        scratch_shapes=[
            pltpu.VMEM((NB,) + shard, BF),
            pltpu.VMEM((NB, BLK), jnp.int32),
            pltpu.VMEM(weight.shape, BF),
            pltpu.VMEM(weight.shape, BF),
            pltpu.VMEM((2, 1, T), jnp.int32),
            pltpu.VMEM((T, BLK, BLK), BF),
            pltpu.VMEM((8, NR * NB), jnp.int32),
            pltpu.SMEM((8, NR * NB), jnp.int32),
            pltpu.VMEM((NR * NB,) + shard, BF),
            pltpu.VMEM((NC, 2) + shard, BF),
            pltpu.VMEM((T + 1,) + shard, F32),
            pltpu.VMEM((NB,) + shard, BF),
            pltpu.VMEM((NC, 2) + shard, BF),
            pltpu.VMEM((NC, 2) + shard, BF),
            pltpu.VMEM((NC, 2) + shard, BF),
            pltpu.VMEM((NB,) + shard, BF),
            pltpu.VMEM((T + 1,) + shard, BF),
            pltpu.VMEM((NR * NB,) + shard, BF),
            pltpu.VMEM((NC, FS, f), BF),
            pltpu.VMEM((4, 3 * NB) + shard, BF),
            pltpu.VMEM((4, NB) + shard, BF),
            pltpu.VMEM((5, NB) + shard, BF),
            pltpu.VMEM((3 * NB,) + shard, BF),
            pltpu.VMEM((NY - 1, 4, FS, f), BF),
            pltpu.VMEM((4, FS, f), BF),
            pltpu.VMEM((2, FS, f), BF),
            pltpu.VMEM((2, FS, f), BF),
            pltpu.VMEM((FS, f), BF),
            pltpu.VMEM((FS, f), BF),
            pltpu.VMEM((NX - 1, FS, f), BF),
            pltpu.VMEM((FS, f), BF),
            pltpu.VMEM((NZ - 1, FS, f), BF),
            pltpu.SemaphoreType.DMA((N_COPIES,)),
            pltpu.SemaphoreType.DMA((N_COPIES,)),
            pltpu.SemaphoreType.DMA((16,)),
        ],
        compiler_params=pltpu.CompilerParams(
            collective_id=0, has_side_effects=True, vmem_limit_bytes=60 << 20
        ),
    )(
        features,
        cotangent,
        weight,
        degree,
        tile_row.reshape(1, T),
        tile_col.reshape(1, T),
        tile_count,
        tile_weights,
    )


def solution(mesh):
    in_specs = (
        P("rows", "cols", None),
        P("rows", "cols", None),
        P(),
        P("rows", None),
        P("rows"),
        P("rows"),
        P("rows"),
        P("rows", None, None),
    )
    out_specs = (P("rows", "cols", None), P("rows", "cols", None), P("cols", None))
    return jax.shard_map(body, mesh=mesh, in_specs=in_specs, out_specs=out_specs, check_vma=False)
```

time: 141 us -> 130 us (0.922)
  local copies, waits for them, and re-layouts: 11.2 us -> 4.81 us
  Pallas kernels: 128 us -> 123 us
    unnamed x29 -> x3, local copies, waits for them, and re-layouts: 11.2 us -> 4.81 us
    pallas_call x5 -> x1, Pallas kernels: 128 us -> 123 us  [body(): pl.pallas_call(layer_kernel, name='layer', out_shape=(jax.ShapeDtypeStruc...]
where the time goes in v2:
time: 130 us; the launch traced here: 129 us
  Pallas kernels  123 us (95%)
  local copies, waits for them, and re-layouts  4.81 us (4%)
    pallas_call x1, Pallas kernels, body(): pl.pallas_call(layer_kernel, name='layer', out_shape=(jax.ShapeDtypeStruc...  123 us
    unnamed x3, local copies, waits for them, and re-layouts  4.81 us

profile of v2, /device:TPU:33, one launch (start us, length us, event | category | flops | bytes accessed | tf_op | source)
XLA Modules:
  0.0 129.3 jit_solution(6921547368221896509)
XLA Ops:
  1.3 123.2 %layer.1 = (bf16[32,32,128]{2,1,0:T(8,128)(2,1)}, bf16[32,32,128]{2,1,0:T(8,128)(2,1)}, f32[32,512]{1,0:T(8,128)}) custom-call(bf16[32,32,128]{2,1,0:T(8,128)(2,1)} %feat.1, bf16[32,32,128]{2,1,0:T(8,128)(2,1)} %cot.1, bf16[512,512]{1,0:T(8,128)(2,1)} %w_h.1, s32[32,128]{1,0:T(8,128)} %deg_h.1, s32[1,256]{1,0:T(1,128)} %bitcast.2, s32[1,256]{1,0:T(1,128)} %bitcast.3, ...), custom_call_target="tpu_custom_call" | custom-call | tf_op jit(solution)/shard_map/layer/pallas_call | solution.py:478
  124.5 1.7 %copy.15 = bf16[32,32,128]{2,1,0:T(8,128)(2,1)} copy(bf16[32,32,128]{2,1,0:T(8,128)(2,1)} %get-tuple-element.6) | data formatting | bytes 524288
  126.2 1.7 %copy.16 = bf16[32,32,128]{2,1,0:T(8,128)(2,1)} copy(bf16[32,32,128]{2,1,0:T(8,128)(2,1)} %get-tuple-element.7) | data formatting | bytes 524288
  127.9 1.5 %copy.17 = f32[32,512]{1,0:T(8,128)} copy(f32[32,512]{1,0:T(8,128)} %get-tuple-element.8) | data formatting | bytes 131072

commit v3 on v2

--- a/solution.py
+++ b/solution.py
@@ -18,6 +18,8 @@
 NY = 4
 NC = 16
 ZFIRST = 26
+XFIRST = 26
+TC = 64
 TB = 16
 T = 256
 DEAD = 1024
@@ -73,7 +75,15 @@
 
 def other_cols():
     c = lax.axis_index("cols")
-    return [{"cols": (c + k) % NC} for k in range(1, NC)]
+    y, z, core = c // 4, (c // 2) % 2, c % 2
+    found = []
+    for dy in (2, 1, 3, 0):
+        for dz in (1, 0):
+            for dc in (1, 0):
+                if (dy, dz, dc) != (0, 0, 0):
+                    k = ((y + dy) % NY) * 4 + (z + dz - 2 * z * dz) * 2 + core + dc - 2 * core * dc
+                    found.append((k, {"cols": k}))
+    return found
 
 
 PERM, COLP, KEYP, ROW, COL, COLEND, ROWEND = range(7)
@@ -118,7 +128,7 @@
 def layer_kernel(
     feat, cot, w_h, deg_h, row_h, col_h, count, a_h,
     act, out, wout,
-    fbuf, deg, w, wt, rowcol, a, idx_v, idx, gat, cotx, sums, hid, hx, act_s, back_s, back, runs, part, wg,
+    fbuf, deg, w, wt, rowcol, a, at, idx_v, idx, gat, cotx, sums, hid, hx, act_s, back_s, back, runs, part, wg,
     inner, summed, half, tail, wy, ws, wc, wm, wz, w1, wx, w2, wv,
     send, recv, lsem,
 ):
@@ -132,7 +142,7 @@
     zpeer = {"cols": c + 2 - 4 * zl}
     xs = [{"rows": rank_along("x", k)} for k in range(1, NX)]
     zs = [{"rows": rank_along("z", k)} for k in range(1, NZ)]
-    peers = devs + xs + zs
+    peers = [d for _, d in devs] + xs + zs
     greet(peers)
     loads = []
 
@@ -217,16 +227,29 @@
     gq.first_start()
     for i in range(PC):
         gp.second_start(0, i)
-    for k, dev in enumerate(devs, 1):
-        last.append(copies.start(cot.at[pl.ds(2 * ((c + k) % NC), 2)], cotx.at[c], dev))
+    for k, dev in devs:
+        last.append(copies.start(cot.at[pl.ds(2 * k, 2)], cotx.at[c], dev))
     for cp in l_idx:
         cp.wait()
     tile_order(rowcol, count, idx_v)
     l_s = load(idx_v, idx)
     l_w.wait()
     wt[...] = w[...].T
+
+    def turn(q):
+        l_a[q].wait()
+
+        def some(i, carry):
+            for k in range(4):
+                t = q * TC + i * 4 + k
+                at[t] = a[t].T
+            return carry
+
+        lax.fori_loop(0, TC // 4, some, 0)
+
     for j in range(QC):
         gq.first_forward(j)
+    turn(0)
     for j in range(PC):
         gp.first_forward(j, gp.second_start)
     for i in range(QC):
@@ -236,11 +259,14 @@
     for j in range(QC):
         gq.second_start(-1, gq.up_order[j])
         gq.second_start(1, gq.dn_order[j])
+    turn(1)
     for j in range((PC + 1) // 2):
         gp.far(j, gp.second_start)
+    turn(2)
     for i in range(PC):
         gp.second_forward(-1, i)
         gp.second_forward(1, PC - 1 - i)
+    turn(3)
     for i in range(QC):
         gq.second_forward(0, i)
     for j in range((QC + 1) // 2):
@@ -256,7 +282,7 @@
         gq.second_forward(2, gq.dn_half[j])
     for cp in last:
         cp.wait_recv()
-    for cp in l_a + [l_s, l_cot]:
+    for cp in [l_s, l_cot]:
         cp.wait()
 
     sums[T] = jnp.zeros((FS, BLK), F32)
@@ -265,7 +291,7 @@
         for k in range(TB):
             p = i * TB + k
             m = lax.dot_general(
-                gat[idx[COLP, p]], a[idx[PERM, p]], (((1,), (1,)), ((), ())), preferred_element_type=F32
+                gat[idx[COLP, p]], at[idx[PERM, p]], (((1,), (0,)), ((), ())), preferred_element_type=F32
             )
             same = idx[KEYP, p] == idx[KEYP, jnp.maximum(p - 1, 0)]
             run = jnp.where(same, run, 0.0) + m
@@ -281,8 +307,8 @@
     lax.fori_loop(0, NB, finish_row, 0, unroll=4)
 
     arrivals = [
-        copies.start(hid.at[pl.ds(2 * ((c + k) % NC), 2)], hx.at[c], dev)
-        for k, dev in enumerate(devs, 1)
+        copies.start(hid.at[pl.ds(2 * k, 2)], hx.at[c], dev)
+        for k, dev in devs
     ]
     hx[c] = hid[pl.ds(2 * c, 2)]
     runs[T] = jnp.zeros((FS, BLK), BF)
@@ -298,8 +324,8 @@
 
     def to_owner(src, dst):
         got = [
-            copies.start(src.at[(c + k) % NC], dst.at[pl.ds(2 * c, 2)], dev)
-            for k, dev in enumerate(devs, 1)
+            copies.start(src.at[k], dst.at[pl.ds(2 * c, 2)], dev)
+            for k, dev in devs
         ]
         return got, load(src.at[c], dst.at[pl.ds(2 * c, 2)])
 
@@ -311,16 +337,11 @@
     narrow(back_s, (jnp.dot(w[...], slope, preferred_element_type=F32) * s).astype(BF))
     got_b, mine_b = to_owner(back_s, back)
     narrow(act_s, (pre * sig).astype(BF))
-    got_a, mine_a = to_owner(act_s, act)
     wg[...] = (
         lax.dot_general(x, slope, (((1,), (1,)), ((), ())), preferred_element_type=F32)
         .astype(BF)
         .reshape(wg.shape)
     )
-    wys = [
-        copies.start(wg.at[pl.ds(4 * ((y + k) % NY), 4)], wy.at[k - 1], d)
-        for k, d in enumerate(ypeers, 1)
-    ]
     for cp in got_b:
         cp.wait_recv()
     mine_b.wait()
@@ -336,111 +357,178 @@
 
     lax.fori_loop(0, T // TB, backward, jnp.zeros((FS, BLK), F32))
 
-    def pick(i, carry):
-        part[i] = runs[idx[COLEND, i]]
-        return carry
-
-    lax.fori_loop(0, NR * NB, pick, 0, unroll=8)
-
-    class Shards:
-        def __init__(self, first, second, lo, n):
-            self.f, self.s, self.lo, self.n = first, second, lo, n
-
-        def local(self, a, b):
-            return part.at[pl.ds(owner_at(self.f, a, self.s, b) * NB + self.lo, self.n)]
-
-    def ring_start(axis, n, shard, land):
-        h = n // 2
-        up, dn = {"rows": rank_along(axis, 1)}, {"rows": rank_along(axis, -1)}
+    def local(first, a, second, b, lo, n):
+        return part.at[pl.ds(owner_at(first, a, second, b) * NB + lo, n)]
+
+    def add_into(dst, p, q):
+        def one(i, carry):
+            dst[i] = (p[i].astype(F32) + q[i].astype(F32)).astype(BF)
+            return carry
+
+        lax.fori_loop(0, dst.shape[0], one, 0, unroll=2)
+
+    class Ring:
+        def __init__(self, axis, n, shard, land, work):
+            self.n, self.h, self.shard, self.land, self.work = n, n // 2, shard, land, work
+            self.up, self.dn = {"rows": rank_along(axis, 1)}, {"rows": rank_along(axis, -1)}
+            self.got = []
+
+        def far(self):
+            n, h = self.n, self.h
+            self.far_dn = copies.start(self.shard(-2).at[pl.ds(0, h)], self.land.at[pl.ds(0, h)], self.dn)
+            self.far_up = copies.start(
+                self.shard(2).at[pl.ds(h, n - h)], self.land.at[pl.ds(h, n - h)], self.up
+            )
+
+        def raw_dn(self):
+            n, h = self.n, self.h
+            self.got.append(
+                copies.start(self.shard(-1).at[pl.ds(h, n - h)], self.land.at[pl.ds(n + h, n - h)], self.dn)
+            )
+
+        def raw_up(self):
+            n, h = self.n, self.h
+            self.got.append(
+                copies.start(self.shard(1).at[pl.ds(0, h)], self.land.at[pl.ds(2 * n, h)], self.up)
+            )
+
+        def start(self):
+            self.far()
+            self.raw_dn()
+            self.raw_up()
+
+        def forward(self):
+            n, h = self.n, self.h
+            lo, hi = pl.ds(0, h), pl.ds(h, n - h)
+            self.far_dn.wait_recv()
+            add_into(self.work.at[lo], self.land.at[lo], self.shard(-1).at[lo])
+            self.got.append(copies.start(self.work.at[lo], self.land.at[pl.ds(n, h)], self.dn))
+            self.far_up.wait_recv()
+            add_into(self.work.at[hi], self.land.at[hi], self.shard(1).at[hi])
+            self.got.append(copies.start(self.work.at[hi], self.land.at[pl.ds(2 * n + h, n - h)], self.up))
+
+        def end(self, store):
+            n, land = self.n, self.land
+            for cp in self.got:
+                cp.wait_recv()
+            mine = self.shard(0)
+
+            def one(i, carry):
+                store(i, mine[i].astype(F32) + land[n + i].astype(F32) + land[2 * n + i].astype(F32))
+                return carry
+
+            lax.fori_loop(0, n, one, 0, unroll=2)
+
+    slot = {2: 0, -2: 0, -1: 1, 1: 2, 0: 3}
+
+    def first_rings(first, second, lo, n):
         return {
-            "n": n,
-            "up": up,
-            "dn": dn,
-            "shard": shard,
-            "land": land,
-            "far_dn": copies.start(shard(-2).at[pl.ds(0, h)], land.at[pl.ds(0, h)], dn),
-            "far_up": copies.start(shard(2).at[pl.ds(h, n - h)], land.at[pl.ds(h, n - h)], up),
-            "raw_dn": copies.start(shard(-1).at[pl.ds(h, n - h)], land.at[pl.ds(n + h, n - h)], dn),
-            "raw_up": copies.start(shard(1).at[pl.ds(0, h)], land.at[pl.ds(2 * n, h)], up),
+            b: Ring(
+                first,
+                n,
+                lambda a, b=b: local(first, a, second, b, lo, n),
+                inner.at[slot[b], pl.ds(3 * lo, 3 * n)],
+                half.at[slot[b], pl.ds(lo, n)],
+            )
+            for b in (2, -1, 1, 0)
         }
 
-    def add_into(dst, a, b):
+    def second_ring(second, lo, n):
+        return Ring(
+            second,
+            n,
+            lambda a: summed.at[slot[a], pl.ds(lo, n)],
+            tail.at[pl.ds(3 * lo, 3 * n)],
+            half.at[4, pl.ds(lo, n)],
+        )
+
+    def keep(b, lo):
+        def store(j, v):
+            summed[slot[b], lo + j] = v.astype(BF)
+
+        return store
+
+    def final(lo):
+        def store(j, v):
+            out[lo + j] = (v * scale_of(lo + j)).astype(BF)
+
+        return store
+
+    PN, QN = XFIRST, NB - XFIRST
+    p1, p2 = first_rings("x", "z", 0, PN), second_ring("z", 0, PN)
+    q1, q2 = first_rings("z", "x", PN, QN), second_ring("x", PN, QN)
+
+    def pick(dx, dz, lo, n):
+        first = owner_at("x", dx, "z", dz) * NB + lo
+
         def one(i, carry):
-            dst[i] = (a[i].astype(F32) + b[i].astype(F32)).astype(BF)
+            part[first + i] = runs[idx[COLEND, first + i]]
             return carry
 
-        lax.fori_loop(0, dst.shape[0], one, 0, unroll=2)
-
-    def ring_forward(r, work):
-        n, land = r["n"], r["land"]
-        h = n // 2
-        r["far_dn"].wait_recv()
-        add_into(work.at[pl.ds(0, h)], land.at[pl.ds(0, h)], r["shard"](-1).at[pl.ds(0, h)])
-        r["sum_dn"] = copies.start(work.at[pl.ds(0, h)], land.at[pl.ds(n, h)], r["dn"])
-        r["far_up"].wait_recv()
-        add_into(
-            work.at[pl.ds(h, n - h)], land.at[pl.ds(h, n - h)], r["shard"](1).at[pl.ds(h, n - h)]
-        )
-        r["sum_up"] = copies.start(work.at[pl.ds(h, n - h)], land.at[pl.ds(2 * n + h, n - h)], r["up"])
-
-    def ring_end(r, store):
-        n, land = r["n"], r["land"]
-        for name in ("raw_dn", "raw_up", "sum_dn", "sum_up"):
-            r[name].wait_recv()
-        mine = r["shard"](0)
-
-        def one(i, carry):
-            store(i, mine[i].astype(F32) + land[n + i].astype(F32) + land[2 * n + i].astype(F32))
-            return carry
-
-        lax.fori_loop(0, n, one, 0, unroll=2)
-
-    order = (2, -1, 1, 0)
-    gp = Shards("x", "z", 0, ZFIRST)
-    gq = Shards("z", "x", ZFIRST, NB - ZFIRST)
-    rings = {}
-    for i, b in enumerate(order):
-        for g in (gp, gq):
-            shard = lambda a, g=g, b=b: g.local(a, b)
-            land = inner.at[i, pl.ds(3 * g.lo, 3 * g.n)]
-            rings[g, b] = ring_start(g.f, g.n, shard, land)
-
-    def keep(g, i):
-        def store(j, v):
-            summed[i, g.lo + j] = v.astype(BF)
-
-        return store
-
-    for i, b in enumerate(order):
-        for g in (gp, gq):
-            ring_forward(rings[g, b], half.at[i, pl.ds(g.lo, g.n)])
-        if i == 1:
-            for cp in wys:
-                cp.wait_recv()
-            for j in range(4):
-                v = wg[4 * y + j].astype(F32)
-                for k in range(NY - 1):
-                    v = v + wy[k, j].astype(F32)
-                ws[j] = v.astype(BF)
-            wcs = [copies.start(ws.at[2 * q + 1 - core], wc.at[q], cpeer) for q in range(2)]
-    second = {}
-    for i, b in enumerate(order):
-        for g in (gp, gq):
-            ring_end(rings[g, b], keep(g, i))
+        lax.fori_loop(0, n, one, 0, unroll=True)
+
+    away = (2, -1, 1, 0)
+    for dx in away:
+        pick(dx, 2, 0, PN)
+    p1[2].start()
+    for dz in away:
+        for dx in away:
+            pick(dx, dz, PN, QN)
+    for b in away:
+        q1[b].start()
+    for dx in away:
+        pick(dx, -1, 0, PN)
+    p1[-1].start()
+    for dz in (1, 0):
+        for dx in away:
+            pick(dx, dz, 0, PN)
+    got_a, mine_a = to_owner(act_s, act)
+    wys = [
+        copies.start(wg.at[pl.ds(4 * ((y + k) % NY), 4)], wy.at[k - 1], d)
+        for k, d in enumerate(ypeers, 1)
+    ]
+    p1[2].forward()
+    p1[1].start()
+    q1[2].forward()
+    p1[2].end(keep(2, 0))
+    p2.far()
+    p1[-1].forward()
+    p1[0].start()
+    q1[-1].forward()
+    q1[1].forward()
+    q1[0].forward()
+    for cp in wys:
+        cp.wait_recv()
+    for j in range(4):
+        v = wg[4 * y + j].astype(F32)
+        for k in range(NY - 1):
+            v = v + wy[k, j].astype(F32)
+        ws[j] = v.astype(BF)
+    wcs = [copies.start(ws.at[2 * q + 1 - core], wc.at[q], cpeer) for q in range(2)]
+    p1[-1].end(keep(-1, 0))
+    p2.raw_dn()
+    p1[1].forward()
+    q1[2].end(keep(2, PN))
+    q2.far()
+    q1[-1].end(keep(-1, PN))
+    q2.raw_dn()
+    q1[1].end(keep(1, PN))
+    q2.raw_up()
     for cp in wcs:
         cp.wait_recv()
     for q in range(2):
         wm[q] = (ws[2 * q + core].astype(F32) + wc[q].astype(F32)).astype(BF)
     wzc = copies.start(wm.at[1 - zl], wz, zpeer)
-    place = {2: 0, -2: 0, -1: 1, 1: 2, 0: 3}
-    for g in (gp, gq):
-        shard = lambda a, g=g: summed.at[place[a], pl.ds(g.lo, g.n)]
-        second[g] = ring_start(g.s, g.n, shard, tail.at[pl.ds(3 * g.lo, 3 * g.n)])
+    q1[0].end(keep(0, PN))
+    p1[1].end(keep(1, 0))
+    p2.raw_up()
+    p2.forward()
+    q2.forward()
+    p1[0].forward()
     wzc.wait_recv()
     w1[...] = (wm[zl].astype(F32) + wz[...].astype(F32)).astype(BF)
     wxs = [copies.start(w1, wx.at[k], d) for k, d in enumerate(xs)]
-    for g in (gp, gq):
-        ring_forward(second[g], half.at[4, pl.ds(g.lo, g.n)])
+    q2.end(final(PN))
     for cp in wxs:
         cp.wait_recv()
     v = w1[...].astype(F32)
@@ -448,12 +536,8 @@
         v = v + wx[k].astype(F32)
     w2[...] = v.astype(BF)
     wvs = [copies.start(w2, wv.at[k], d) for k, d in enumerate(zs)]
-    for g in (gp, gq):
-
-        def final(j, v, g=g):
-            out[g.lo + j] = (v * scale_of(g.lo + j)).astype(BF)
-
-        ring_end(second[g], final)
+    p1[0].end(keep(0, 0))
+    p2.end(final(0))
     for cp in wvs:
         cp.wait_recv()
     v = w2[...].astype(F32)
@@ -464,6 +548,31 @@
         cp.wait_recv()
     mine_a.wait()
     copies.finish()
+
+
+def hand_over_kernel(a_in, b_in, c_in, a_out, b_out, c_out, sem):
+    moves = [
+        pltpu.make_async_copy(src, dst, sem.at[i])
+        for i, (src, dst) in enumerate(((a_in, a_out), (b_in, b_out), (c_in, c_out)))
+    ]
+    for m in moves:
+        m.start()
+    for m in moves:
+        m.wait()
+
+
+def hand_over(results):
+    vm = pl.BlockSpec(memory_space=pltpu.VMEM)
+    hb = pl.BlockSpec(memory_space=pl.ANY)
+    return pl.pallas_call(
+        hand_over_kernel,
+        name="hand_over",
+        out_shape=tuple(jax.ShapeDtypeStruct(r.shape, r.dtype) for r in results),
+        in_specs=[vm] * 3,
+        out_specs=(hb,) * 3,
+        scratch_shapes=[pltpu.SemaphoreType.DMA((3,))],
+        compiler_params=pltpu.CompilerParams(vmem_limit_bytes=60 << 20),
+    )(*results)
 
 
 N_COPIES = 2 * 2 * 15 + 4 * (NC - 1) + 2 * (4 * 6 + 6) + (NY - 1) + 2 + 1 + (NX - 1) + (NZ - 1)
@@ -475,7 +584,7 @@
     sm = pl.BlockSpec(memory_space=pltpu.SMEM)
     f = weight.shape[1]
     shard = (FS, BLK)
-    return pl.pallas_call(
+    results = pl.pallas_call(
         layer_kernel,
         name="layer",
         out_shape=(
@@ -491,6 +600,7 @@
             pltpu.VMEM(weight.shape, BF),
             pltpu.VMEM(weight.shape, BF),
             pltpu.VMEM((2, 1, T), jnp.int32),
+            pltpu.VMEM((T, BLK, BLK), BF),
             pltpu.VMEM((T, BLK, BLK), BF),
             pltpu.VMEM((8, NR * NB), jnp.int32),
             pltpu.SMEM((8, NR * NB), jnp.int32),
@@ -535,6 +645,7 @@
         tile_count,
         tile_weights,
     )
+    return hand_over(results)
 
 
 def solution(mesh):

time: 130 us -> 113 us (0.87)
  Pallas kernels: 123 us -> 111 us
  local copies, waits for them, and re-layouts: 4.81 us -> 0 us
    pallas_call x1, Pallas kernels: 123 us -> 109 us  [body(): pl.pallas_call(layer_kernel, name='layer', out_shape=(jax.ShapeDtypeStruc...]
    unnamed x3 -> x0, local copies, waits for them, and re-layouts: 4.81 us -> none
    pallas_call x0 -> x1, Pallas kernels: none -> 1.86 us  [hand_over(): pl.pallas_call(hand_over_kernel, name='hand_over', out_shape=tuple((jax.S...]
where the time goes in v3:
time: 113 us; the launch traced here: 112 us
  Pallas kernels  111 us (98%)
  between operations  1.29 us (1%)
    pallas_call x1, Pallas kernels, body(): pl.pallas_call(layer_kernel, name='layer', out_shape=(jax.ShapeDtypeStruc...  109 us

profile of v3, /device:TPU:33, one launch (start us, length us, event | category | flops | bytes accessed | tf_op | source)
XLA Modules:
  0.0 112.1 jit_solution(16947851271946412736)
XLA Ops:
  1.3 108.9 %layer.1 = (bf16[32,32,128]{2,1,0:T(8,128)(2,1)}, bf16[32,32,128]{2,1,0:T(8,128)(2,1)}, f32[32,512]{1,0:T(8,128)}) custom-call(bf16[32,32,128]{2,1,0:T(8,128)(2,1)} %feat.1, bf16[32,32,128]{2,1,0:T(8,128)(2,1)} %cot.1, bf16[512,512]{1,0:T(8,128)(2,1)} %w_h.1, s32[32,128]{1,0:T(8,128)} %deg_h.1, s32[1,256]{1,0:T(1,128)} %bitcast.2, s32[1,256]{1,0:T(1,128)} %bitcast.3, ...), custom_call_target="tpu_custom_call" | custom-call | tf_op jit(solution)/shard_map/layer/pallas_call | solution.py:587
  110.2 1.9 %hand_over.1 = (bf16[32,32,128]{2,1,0:T(8,128)(2,1)}, bf16[32,32,128]{2,1,0:T(8,128)(2,1)}, f32[32,512]{1,0:T(8,128)}) custom-call(bf16[32,32,128]{2,1,0:T(8,128)(2,1)} %get-tuple-element.6.a_in, bf16[32,32,128]{2,1,0:T(8,128)(2,1)} %get-tuple-element.7.b_in, f32[32,512]{1,0:T(8,128)} %get-tuple-element.8.c_in), custom_call_target="tpu_custom_call" | custom-call | tf_op jit(solution)/shard_map/hand_over/pallas_call | solution.py:567

commit v4 on v3

--- a/solution.py
+++ b/solution.py
@@ -20,7 +20,7 @@
 ZFIRST = 26
 XFIRST = 26
 TC = 64
-TB = 16
+TB = 64
 T = 256
 DEAD = 1024
 
@@ -455,8 +455,7 @@
         return store
 
     PN, QN = XFIRST, NB - XFIRST
-    p1, p2 = first_rings("x", "z", 0, PN), second_ring("z", 0, PN)
-    q1, q2 = first_rings("z", "x", PN, QN), second_ring("x", PN, QN)
+    away = (2, -1, 1, 0)
 
     def pick(dx, dz, lo, n):
         first = owner_at("x", dx, "z", dz) * NB + lo
@@ -467,83 +466,111 @@
 
         lax.fori_loop(0, n, one, 0, unroll=True)
 
-    away = (2, -1, 1, 0)
+    rings, seconds = [], []
+    for lo, n in ((0, 13), (13, 13)):
+        one = first_rings("x", "z", lo, n)
+        seconds.append(second_ring("z", lo, n))
+        rings += [(one[b], b, lo, seconds[-1]) for b in away]
+    q1, q2 = first_rings("z", "x", PN, QN), second_ring("x", PN, QN)
+
+    def end_first(ring, b, lo, second):
+        ring.end(keep(b, lo))
+        if b == 2:
+            second.far()
+        if b == -1:
+            second.raw_dn()
+        if b == 1:
+            second.raw_up()
+
+    AHEAD = 3
     for dx in away:
         pick(dx, 2, 0, PN)
-    p1[2].start()
+    rings[0][0].start()
     for dz in away:
         for dx in away:
             pick(dx, dz, PN, QN)
     for b in away:
         q1[b].start()
-    for dx in away:
-        pick(dx, -1, 0, PN)
-    p1[-1].start()
-    for dz in (1, 0):
+    for dz in away[1:]:
         for dx in away:
             pick(dx, dz, 0, PN)
+    for k in range(1, AHEAD):
+        rings[k][0].start()
     got_a, mine_a = to_owner(act_s, act)
     wys = [
         copies.start(wg.at[pl.ds(4 * ((y + k) % NY), 4)], wy.at[k - 1], d)
         for k, d in enumerate(ypeers, 1)
     ]
-    p1[2].forward()
-    p1[1].start()
-    q1[2].forward()
-    p1[2].end(keep(2, 0))
-    p2.far()
-    p1[-1].forward()
-    p1[0].start()
-    q1[-1].forward()
-    q1[1].forward()
-    q1[0].forward()
-    for cp in wys:
-        cp.wait_recv()
-    for j in range(4):
-        v = wg[4 * y + j].astype(F32)
-        for k in range(NY - 1):
-            v = v + wy[k, j].astype(F32)
-        ws[j] = v.astype(BF)
-    wcs = [copies.start(ws.at[2 * q + 1 - core], wc.at[q], cpeer) for q in range(2)]
-    p1[-1].end(keep(-1, 0))
-    p2.raw_dn()
-    p1[1].forward()
-    q1[2].end(keep(2, PN))
-    q2.far()
-    q1[-1].end(keep(-1, PN))
-    q2.raw_dn()
-    q1[1].end(keep(1, PN))
-    q2.raw_up()
-    for cp in wcs:
-        cp.wait_recv()
-    for q in range(2):
-        wm[q] = (ws[2 * q + core].astype(F32) + wc[q].astype(F32)).astype(BF)
-    wzc = copies.start(wm.at[1 - zl], wz, zpeer)
-    q1[0].end(keep(0, PN))
-    p1[1].end(keep(1, 0))
-    p2.raw_up()
-    p2.forward()
-    q2.forward()
-    p1[0].forward()
-    wzc.wait_recv()
-    w1[...] = (wm[zl].astype(F32) + wz[...].astype(F32)).astype(BF)
-    wxs = [copies.start(w1, wx.at[k], d) for k, d in enumerate(xs)]
-    q2.end(final(PN))
-    for cp in wxs:
-        cp.wait_recv()
-    v = w1[...].astype(F32)
-    for k in range(NX - 1):
-        v = v + wx[k].astype(F32)
-    w2[...] = v.astype(BF)
-    wvs = [copies.start(w2, wv.at[k], d) for k, d in enumerate(zs)]
-    p1[0].end(keep(0, 0))
-    p2.end(final(0))
+
+    def sum_y():
+        for cp in wys:
+            cp.wait_recv()
+        for j in range(4):
+            v = wg[4 * y + j].astype(F32)
+            for k in range(NY - 1):
+                v = v + wy[k, j].astype(F32)
+            ws[j] = v.astype(BF)
+        return [copies.start(ws.at[2 * q + 1 - core], wc.at[q], cpeer) for q in range(2)]
+
+    def sum_core():
+        for cp in wcs:
+            cp.wait_recv()
+        for q in range(2):
+            wm[q] = (ws[2 * q + core].astype(F32) + wc[q].astype(F32)).astype(BF)
+        return copies.start(wm.at[1 - zl], wz, zpeer)
+
+    def sum_near():
+        wzc.wait_recv()
+        w1[...] = (wm[zl].astype(F32) + wz[...].astype(F32)).astype(BF)
+        return [copies.start(w1, wx.at[k], d) for k, d in enumerate(xs)]
+
+    def sum_x():
+        for cp in wxs:
+            cp.wait_recv()
+        v = w1[...].astype(F32)
+        for k in range(NX - 1):
+            v = v + wx[k].astype(F32)
+        w2[...] = v.astype(BF)
+        return [copies.start(w2, wv.at[k], d) for k, d in enumerate(zs)]
+
+    for i in range(len(rings)):
+        rings[i][0].forward()
+        if i + AHEAD < len(rings):
+            rings[i + AHEAD][0].start()
+        if i >= 1:
+            end_first(*rings[i - 1])
+            if rings[i - 1][1] == 1:
+                rings[i - 1][3].forward()
+        if i == 0:
+            q1[2].forward()
+        if i == 1:
+            q1[-1].forward()
+            q1[1].forward()
+            q1[0].forward()
+        if i == 2:
+            wcs = sum_y()
+        if i == 3:
+            wzc = sum_core()
+            end_first(q1[2], 2, PN, q2)
+        if i == 4:
+            end_first(q1[-1], -1, PN, q2)
+            end_first(q1[1], 1, PN, q2)
+            q1[0].end(keep(0, PN))
+            wxs = sum_near()
+        if i == 5:
+            q2.forward()
+            wvs = sum_x()
+        if i == 6:
+            seconds[0].end(final(0))
+            q2.end(final(PN))
     for cp in wvs:
         cp.wait_recv()
     v = w2[...].astype(F32)
     for k in range(NZ - 1):
         v = v + wv[k].astype(F32)
     wout[...] = v
+    end_first(*rings[-1])
+    seconds[1].end(final(13))
     for cp in got_a:
         cp.wait_recv()
     mine_a.wait()
@@ -575,7 +602,7 @@
     )(*results)
 
 
-N_COPIES = 2 * 2 * 15 + 4 * (NC - 1) + 2 * (4 * 6 + 6) + (NY - 1) + 2 + 1 + (NX - 1) + (NZ - 1)
+N_COPIES = 2 * 2 * 15 + 4 * (NC - 1) + 3 * (4 * 6 + 6) + (NY - 1) + 2 + 1 + (NX - 1) + (NZ - 1)
 
 
 def body(features, cotangent, weight, degree, tile_row, tile_col, tile_count, tile_weights):

time: 113 us -> 109 us (0.965)
  Pallas kernels: 111 us -> 107 us
    pallas_call x1, Pallas kernels: 109 us -> 106 us  [body(): pl.pallas_call(layer_kernel, name='layer', out_shape=(jax.ShapeDtypeStruc...]
where the time goes in v4:
time: 109 us
  Pallas kernels  107 us (98%)
  between operations  1.29 us (1%)
    pallas_call x1, Pallas kernels, body(): pl.pallas_call(layer_kernel, name='layer', out_shape=(jax.ShapeDtypeStruc...  106 us

profile of v4, /device:TPU:33, one launch (start us, length us, event | category | flops | bytes accessed | tf_op | source)
XLA Modules:
  0.0 108.8 jit_solution(13723906937088688286)
XLA Ops:
  1.3 105.6 %layer.1 = (bf16[32,32,128]{2,1,0:T(8,128)(2,1)}, bf16[32,32,128]{2,1,0:T(8,128)(2,1)}, f32[32,512]{1,0:T(8,128)}) custom-call(bf16[32,32,128]{2,1,0:T(8,128)(2,1)} %feat.1, bf16[32,32,128]{2,1,0:T(8,128)(2,1)} %cot.1, bf16[512,512]{1,0:T(8,128)(2,1)} %w_h.1, s32[32,128]{1,0:T(8,128)} %deg_h.1, s32[1,256]{1,0:T(1,128)} %bitcast.2, s32[1,256]{1,0:T(1,128)} %bitcast.3, ...), custom_call_target="tpu_custom_call" | custom-call | tf_op jit(solution)/shard_map/layer/pallas_call | solution.py:614
  106.9 1.9 %hand_over.1 = (bf16[32,32,128]{2,1,0:T(8,128)(2,1)}, bf16[32,32,128]{2,1,0:T(8,128)(2,1)}, f32[32,512]{1,0:T(8,128)}) custom-call(bf16[32,32,128]{2,1,0:T(8,128)(2,1)} %get-tuple-element.6.a_in, bf16[32,32,128]{2,1,0:T(8,128)(2,1)} %get-tuple-element.7.b_in, f32[32,512]{1,0:T(8,128)} %get-tuple-element.8.c_in), custom_call_target="tpu_custom_call" | custom-call | tf_op jit(solution)/shard_map/hand_over/pallas_call | solution.py:594

commit v5 on v4

--- a/solution.py
+++ b/solution.py
@@ -20,7 +20,7 @@
 ZFIRST = 26
 XFIRST = 26
 TC = 64
-TB = 64
+TB = 128
 T = 256
 DEAD = 1024
 

time: 109 us -> 108 us (level)
  no operation moved by 1% of the time
where the time goes in v5:
time: 108 us
  Pallas kernels  107 us (99%)
  between operations  1.29 us (1%)
    pallas_call x1, Pallas kernels, body(): pl.pallas_call(layer_kernel, name='layer', out_shape=(jax.ShapeDtypeStruc...  105 us

profile of v5, /device:TPU:33, one launch (start us, length us, event | category | flops | bytes accessed | tf_op | source)
XLA Modules:
  0.0 108.3 jit_solution(16957779211208198073)
XLA Ops:
  1.3 105.1 %layer.1 = (bf16[32,32,128]{2,1,0:T(8,128)(2,1)}, bf16[32,32,128]{2,1,0:T(8,128)(2,1)}, f32[32,512]{1,0:T(8,128)}) custom-call(bf16[32,32,128]{2,1,0:T(8,128)(2,1)} %feat.1, bf16[32,32,128]{2,1,0:T(8,128)(2,1)} %cot.1, bf16[512,512]{1,0:T(8,128)(2,1)} %w_h.1, s32[32,128]{1,0:T(8,128)} %deg_h.1, s32[1,256]{1,0:T(1,128)} %bitcast.2, s32[1,256]{1,0:T(1,128)} %bitcast.3, ...), custom_call_target="tpu_custom_call" | custom-call | tf_op jit(solution)/shard_map/layer/pallas_call | solution.py:614
  106.4 1.9 %hand_over.1 = (bf16[32,32,128]{2,1,0:T(8,128)(2,1)}, bf16[32,32,128]{2,1,0:T(8,128)(2,1)}, f32[32,512]{1,0:T(8,128)}) custom-call(bf16[32,32,128]{2,1,0:T(8,128)(2,1)} %get-tuple-element.6.a_in, bf16[32,32,128]{2,1,0:T(8,128)(2,1)} %get-tuple-element.7.b_in, f32[32,512]{1,0:T(8,128)} %get-tuple-element.8.c_in), custom_call_target="tpu_custom_call" | custom-call | tf_op jit(solution)/shard_map/hand_over/pallas_call | solution.py:594
